TPU v7x, 128 devices: a whole 4x4x4 slice. The times are simulated.
128 devices in a mesh: replica: 2 (over core), dp: 8 (over y, x_hi), tensor: 8 (over z, x_lo).
Axes of the slice: x: 4 (x_hi: 2, x_lo: 2; x = x_hi * 2 + x_lo), y: 4, z: 4, core: 2. Of those that a mesh axis runs over, the one named last changes fastest.
Arguments:
- tokens: bfloat16 [2, 1024, 4096], P('replica', 'tensor', 'dp'), may hold values from -6 to 6
- cotangent: bfloat16 [2, 1024, 4096], P('replica', 'tensor', 'dp'), may hold values from -0.75 to 0.75
- gate_weight: bfloat16 [2, 4096, 14336], P('replica', 'dp', 'tensor'), may hold values from -0.09375 to 0.09375
- up_weight: bfloat16 [2, 4096, 14336], P('replica', 'dp', 'tensor'), may hold values from -0.09375 to 0.09375
- down_weight: bfloat16 [2, 14336, 4096], P('replica', 'tensor', 'dp'), may hold values from -0.046875 to 0.046875
- frag_delta: bfloat16 [2, 14336, 4096], P('replica', 'tensor', 'dp'), may hold values from -6 to 6
- outer_momentum: float32 [14336, 4096], P('tensor', 'dp'), may hold values from -6 to 6
Outputs:
- mixed: bfloat16 [2, 1024, 4096], P('replica', 'tensor', 'dp')
- input_grad: bfloat16 [2, 1024, 4096], P('replica', 'tensor', 'dp')
- gate_weight_grad: bfloat16 [2, 4096, 14336], P('replica', 'dp', 'tensor')
- up_weight_grad: bfloat16 [2, 4096, 14336], P('replica', 'dp', 'tensor')
- down_weight_grad: bfloat16 [2, 14336, 4096], P('replica', 'tensor', 'dp')
- outer_step: float32 [14336, 4096], P('tensor', 'dp')
- momentum_next: float32 [14336, 4096], P('tensor', 'dp')
All inputs are finite; a program needn't handle non-finite values.
Results may differ from a plain program's by a relative error of at most 0.033.
Values may be sent and summed in bfloat16 or wider, within the bound.
A program may use at most 128 MiB of HBM per device.

v0:
```python
import jax
import jax.numpy as jnp
from jax import lax
from jax.sharding import PartitionSpec as P

momentum_rate = 0.9
outer_rate = 0.7


def shards(tokens, cotangent, gate_weight, up_weight, down_weight, frag_delta, outer_momentum):
    w_gate = gate_weight[0]
    w_up = up_weight[0]
    w_down = down_weight[0]
    tokens_all, slopes_all = (
        lax.all_gather(tokens[0], "tensor", axis=0, tiled=True),
        lax.all_gather(cotangent[0], "tensor", axis=0, tiled=True),
    )
    gate_part = jnp.dot(tokens_all, w_gate, preferred_element_type=jnp.float32)
    up_part = jnp.dot(tokens_all, w_up, preferred_element_type=jnp.float32)
    gate, up = (
        lax.psum(gate_part.astype(jnp.bfloat16), "dp").astype(jnp.float32),
        lax.psum(up_part.astype(jnp.bfloat16), "dp").astype(jnp.float32),
    )
    sigma = jax.nn.sigmoid(gate)
    active = gate * sigma
    hidden = (active * up).astype(jnp.bfloat16)
    mixed = lax.psum_scatter(
        jnp.dot(hidden, w_down, preferred_element_type=jnp.float32).astype(jnp.bfloat16),
        "tensor",
        scatter_dimension=0,
        tiled=True,
    )
    down_grad = jnp.einsum(
        "tf,td->fd", hidden, slopes_all, preferred_element_type=jnp.float32
    ).astype(jnp.bfloat16)
    hidden_part = jnp.einsum("td,fd->tf", slopes_all, w_down, preferred_element_type=jnp.float32)
    hidden_grad = lax.psum(hidden_part.astype(jnp.bfloat16), "dp").astype(jnp.float32)
    gate_slope = (hidden_grad * up * sigma * (1.0 + gate * (1.0 - sigma))).astype(jnp.bfloat16)
    up_slope = (hidden_grad * active).astype(jnp.bfloat16)
    gate_grad = jnp.einsum(
        "td,tf->df", tokens_all, gate_slope, preferred_element_type=jnp.float32
    ).astype(jnp.bfloat16)
    up_grad = jnp.einsum(
        "td,tf->df", tokens_all, up_slope, preferred_element_type=jnp.float32
    ).astype(jnp.bfloat16)
    term = jnp.einsum("tf,df->td", gate_slope, w_gate, preferred_element_type=jnp.float32)
    input_grad = lax.psum_scatter(
        (term + jnp.einsum("tf,df->td", up_slope, w_up, preferred_element_type=jnp.float32)).astype(
            jnp.bfloat16
        ),
        "tensor",
        scatter_dimension=0,
        tiled=True,
    )
    islands = lax.axis_size("replica")
    total = lax.psum(frag_delta[0], "replica").astype(jnp.float32)
    mean_delta = total / islands
    momentum_next = momentum_rate * outer_momentum + mean_delta
    outer_step = outer_rate * (mean_delta + momentum_rate * momentum_next)
    return (
        mixed[None],
        input_grad[None],
        gate_grad[None],
        up_grad[None],
        down_grad[None],
        outer_step,
        momentum_next,
    )


def solution(mesh):
    placed = (
        P("replica", "tensor", "dp"),
        P("replica", "tensor", "dp"),
        P("replica", "dp", "tensor"),
        P("replica", "dp", "tensor"),
        P("replica", "tensor", "dp"),
        P("replica", "tensor", "dp"),
        P("tensor", "dp"),
    )
    return jax.shard_map(
        shards,
        mesh=mesh,
        in_specs=placed,
        out_specs=(
            P("replica", "tensor", "dp"),
            P("replica", "tensor", "dp"),
            P("replica", "dp", "tensor"),
            P("replica", "dp", "tensor"),
            P("replica", "tensor", "dp"),
            P("tensor", "dp"),
            P("tensor", "dp"),
        ),
        check_vma=False,
    )
```

profile of v0, /device:TPU:0, one launch (start us, length us, event | category | flops | bytes accessed | tf_op | source)
XLA Modules:
  0.0 665.5 jit_solution(4671752294360093127)
XLA Ops:
  7.2 0.7 all-gather.5.cloned.1.call-update
  8.0 0.7 all-gather.7.cloned.1.call-update
  8.7 44.0 %all-gather.5.cloned.1.call-done = bf16[1,1024,512]{2,1,0:T(8,128)(2,1)} async-done(((bf16[1,128,512]{2,1,0:T(8,128)(2,1)}), bf16[1,1024,512]{2,1,0:T(8,128)(2,1)}) %all-gather.5.cloned.1.call-update) | async-done | bytes 1048592 | tf_op jit(solution)/shard_map/all_gather | solution.py:15
  52.8 5.3 convolution_convert_fusion.1
  58.0 3.9 convolution_convert_fusion.2
  61.9 32.5 %all-gather.7.cloned.1.call-done = bf16[1,1024,512]{2,1,0:T(8,128)(2,1)} async-done(((bf16[1,128,512]{2,1,0:T(8,128)(2,1)}), bf16[1,1024,512]{2,1,0:T(8,128)(2,1)}) %all-gather.7.cloned.1.call-update) | async-done | bytes 1048592 | tf_op jit(solution)/shard_map/all_gather | solution.py:16
  94.4 5.7 convolution_convert_fusion
  100.2 0.5 all-reduce.4.cloned.1.call-update
  100.7 440.4 %all-reduce.6.cloned.1.call-done = (bf16[1024,1792]{1,0:T(8,128)(2,1)}, bf16[1024,1792]{1,0:T(8,128)(2,1)}, bf16[1024,1792]{1,0:T(8,128)(2,1)}) async-done(((bf16[1024,1792]{1,0:T(8,128)(2,1)}, bf16[1024,1792]{1,0:T(8,128)(2,1)}, bf16[1024,1792]{1,0:T(8,128)(2,1)}), (bf16[1024,1792]{1,0:T(8,128)(2,1)}, bf16[1024,1792]{1,0:T(8,128)(2,1)}, bf16[1024,1792]{1,0:T(8,128)(2,1)})) %all-reduce.6.cloned.1.call-update) | async-done | bytes 11010064 | tf_op jit(solution)/shard_map/psum | solution.py:22
  541.2 8.3 %fusion.3 = (bf16[1024,1792]{1,0:T(8,128)(2,1)S(1)}, bf16[1024,1792]{1,0:T(8,128)(2,1)S(1)}, bf16[1024,1792]{1,0:T(8,128)(2,1)}) fusion(bf16[1024,1792]{1,0:T(8,128)(2,1)} %get-tuple-element.14, bf16[1024,1792]{1,0:T(8,128)(2,1)} %get-tuple-element.16, bf16[1024,1792]{1,0:T(8,128)(2,1)} %get-tuple-element.15), kind=kLoop, calls=%fused_computation.9 | loop fusion | flops 33030144 | bytes 22020096 | tf_op jit(solution)/shard_map/convert_element_type | solution.py:38
  549.5 2.1 fusion.15
  551.6 1.6 copy-done.3
  553.1 3.1 add_convert_fusion
  556.3 0.2 reduce-scatter.3.cloned.1.call-start
  556.5 5.0 fusion.21
  561.6 8.3 %all-reduce.4.cloned.1.call-done = bf16[1792,512]{1,0:T(8,128)(2,1)} async-done(((bf16[1792,512]{1,0:T(8,128)(2,1)}), bf16[1792,512]{1,0:T(8,128)(2,1)}) %all-reduce.4.cloned.1.call-update) | async-done | bytes 1835024 | tf_op jit(solution)/shard_map/psum | solution.py:56
  569.9 7.0 %add_multiply_fusion = (f32[1792,512]{1,0:T(8,128)}, f32[1792,512]{1,0:T(8,128)}) fusion(bf16[1792,512]{1,0:T(8,128)(2,1)} %all-reduce.4.cloned.1.call-done, f32[1792,512]{1,0:T(8,128)} %param.13), kind=kLoop, calls=%fused_computation.18 | loop fusion | flops 6422528 | bytes 12845056 | tf_op jit(solution)/shard_map/mul | solution.py:59
  576.9 2.1 fusion.9
  579.0 2.4 copy.14
  581.4 5.5 fusion.10
  586.9 4.0 copy.15
  590.8 5.4 fusion.11
  596.2 19.4 %reduce-scatter.5.cloned.1.call-done = bf16[128,512]{1,0:T(8,128)(2,1)} async-done(((bf16[1024,512]{1,0:T(8,128)(2,1)}), bf16[128,512]{1,0:T(8,128)(2,1)}) %reduce-scatter.5.cloned.1.call-update) | async-done | bytes 131088 | tf_op jit(solution)/shard_map/reduce_scatter | solution.py:47
  615.6 43.0 %reduce-scatter.3.cloned.1.call-done = bf16[128,512]{1,0:T(8,128)(2,1)} async-done(((bf16[1024,512]{1,0:T(8,128)(2,1)}), bf16[128,512]{1,0:T(8,128)(2,1)}) %reduce-scatter.3.cloned.1.call-update) | async-done | bytes 131088 | tf_op jit(solution)/shard_map/reduce_scatter | solution.py:27
  (27 shorter events, 0.3 us)
Async XLA Ops:
  7.2 45.6 %copy-start = (bf16[1,512,1792]{2,1,0:T(8,128)(2,1)S(1)}, bf16[1,512,1792]{2,1,0:T(8,128)(2,1)}, u32[]{:S(2)}) copy-start(bf16[1,512,1792]{2,1,0:T(8,128)(2,1)} %param.10) | copy-start | bytes 5505028
  7.2 45.6 %all-gather.5.cloned.1.call-start = ((), (), s32[]{:S(2)}) async-start(), calls=%async_computation.5 | async-start | bytes 1179648 | tf_op jit(solution)/shard_map/all_gather | solution.py:15
  7.9 86.5 %all-gather.7.cloned.1.call-start = ((), (), s32[]{:S(2)}) async-start(), calls=%async_computation.6 | async-start | bytes 1179648 | tf_op jit(solution)/shard_map/all_gather | solution.py:16
  8.7 532.5 %all-reduce.6.cloned.1.call-start = ((), (), s32[]{:S(2)}) async-start(), calls=%async_computation.7 | async-start | bytes 22020096 | tf_op jit(solution)/shard_map/psum | solution.py:22
  52.8 5.3 copy-start.5
  52.8 5.3 copy-start.8
  100.1 469.8 %all-reduce.4.cloned.1.call-start = ((), (), s32[]{:S(2)}) async-start(), calls=%async_computation.4 | async-start | bytes 3670016 | tf_op jit(solution)/shard_map/psum | solution.py:56
  100.7 514.9 %reduce-scatter.5.cloned.1.call-start = ((), (), s32[]{:S(2)}) async-start(), calls=%async_computation.3 | async-start | bytes 1179648 | tf_op jit(solution)/shard_map/reduce_scatter | solution.py:47
  549.5 2.1 copy-start.2
  549.5 3.7 copy-start.3
  549.5 3.7 copy-start.6
  553.1 3.4 copy-start.7
  556.3 102.3 %reduce-scatter.3.cloned.1.call-start = ((), (), s32[]{:S(2)}) async-start(), calls=%async_computation.2 | async-start | bytes 1179648 | tf_op jit(solution)/shard_map/reduce_scatter | solution.py:27
  569.9 7.0 %copy-start.4 = (bf16[1024,1792]{1,0:T(8,128)(2,1)S(1)}, bf16[1024,1792]{1,0:T(8,128)(2,1)}, u32[]{:S(2)}) copy-start(bf16[1024,1792]{1,0:T(8,128)(2,1)} %copy-done.3) | copy-start | bytes 11010052
  586.9 4.0 copy-start.9
  586.9 71.7 %copy-start.1 = (bf16[1,512,1792]{2,1,0:T(8,128)(2,1)S(1)}, bf16[1,512,1792]{2,1,0:T(8,128)(2,1)}, u32[]{:S(2)}) copy-start(bf16[1,512,1792]{2,1,0:T(8,128)(2,1)} %param.10) | copy-start | bytes 5505028
Sparse Core Ops, SparseCore 0:
  9.7 43.0 all-gather.4
  54.4 39.9 all-gather.6
  100.2 440.8 all-reduce.5
  543.5 26.4 all-reduce.3
  572.9 42.7 reduce-scatter.4
  618.6 40.0 reduce-scatter.2
where the time goes:
time: 666 us; the launch traced here: 665 us
  waiting for transfers between devices  590 us (89%)
  matrix products  38.1 us (6%)
  other arithmetic  15.3 us (2%)
  between operations  14.2 us (2%)
  local copies, waits for them, and re-layouts  7.94 us (1%)
    psum x1, waiting for transfers between devices, shards(): lax.psum(up_part.astype(jnp.bfloat16), 'dp').astype(jnp.float32)  440 us
    all_gather x1, waiting for transfers between devices, shards(): lax.all_gather(tokens[0], 'tensor', axis=0, tiled=True)  44 us
    reduce_scatter x1, waiting for transfers between devices, shards(): lax.psum_scatter(jnp.dot(hidden, w_down, preferred_element_type=jnp.float...  43 us
    all_gather x1, waiting for transfers between devices, shards(): lax.all_gather(cotangent[0], 'tensor', axis=0, tiled=True)  32.5 us
    reduce_scatter x1, waiting for transfers between devices, shards(): lax.psum_scatter((term + jnp.einsum('tf,df->td', up_slope, w_up, preferre...  19.4 us
  transfers between devices with their start and end apart: 6, of which 6 were waited for; matrix products, arithmetic and copies ran while one was open for 8% of the time, Pallas kernels for 0%

commit v1 on v0

v1 whole, which is shorter than its diff:
```python
import functools

import jax
import jax.numpy as jnp
from jax import lax
from jax.experimental import pallas as pl
from jax.experimental.pallas import tpu as pltpu
from jax.sharding import PartitionSpec as P

MESH = pl.DeviceIdType.MESH
F32 = jnp.float32
BF16 = jnp.bfloat16
momentum_rate = 0.9
outer_rate = 0.7

ROWS = 1024
OWN = 128
DIM = 512
UNITS = 1792
CHUNKS = 4
TC = ROWS // CHUNKS
SLOTS = 2
CY = 1024
CX = UNITS - CY
HY = CY // 2
HX = CX // 2
YB = TC // 4
XR = TC // 2
XB = XR // 4
TILE = 256
Z_ORDER = (0, 3, 1, 2)
SEMS = 160


def tick_order():
    order = []
    for tick in range(CHUNKS + 6):
        for stage, lag in (
            ("F", 5), ("E", 4), ("D", 3), ("C", 2), ("By", 1), ("A", 0), ("Bx", 1), ("G", 6),
        ):
            chunk = tick - lag
            if 0 <= chunk < CHUNKS:
                order += [(part, chunk) for part in PARTS[stage]]
    return order


PARTS = {
    "A": ("A",),
    "By": ("By",),
    "Bx": ("Bx",),
    "C": ("Cy", "Cx"),
    "D": ("Dy", "Dx"),
    "E": ("Ey", "Ex"),
    "F": ("Fy", "Fx"),
    "G": ("G",),
}


def pointwise(gate, up, hidden_grad):
    sigma = jax.nn.sigmoid(gate)
    active = gate * sigma
    hidden = active * up
    gate_slope = hidden_grad * up * sigma * (1.0 + gate * (1.0 - sigma))
    up_slope = hidden_grad * active
    return hidden.astype(BF16), gate_slope.astype(BF16), up_slope.astype(BF16)


def dot(a, b, ca=1, cb=0):
    return lax.dot_general(a, b, (((ca,), (cb,)), ((), ())), preferred_element_type=F32)


def kernel(
    tok_in, cot_in, wg_hbm, wu_hbm, wd_hbm, frag_in,
    mixed_out, ig_out, gg_out, ug_out, dg_out, frag_out,
    wg, wu, wd, tc_all, tc_t, part, h_all, ra, rb, sy, rc, e_own, xa, xb, xc, g_all, ms, rz, rx, gg, ug, dg,
    send_sem, recv_sem, local_sem,
):
    rep, d, t = lax.axis_index("replica"), lax.axis_index("dp"), lax.axis_index("tensor")
    y, xh = lax.div(d, 2), lax.rem(d, 2)
    z, xl = lax.div(t, 2), lax.rem(t, 2)
    x = 2 * xh + xl

    def at(yy, zz, xx):
        return (rep, yy * 2 + lax.div(xx, 2), zz * 2 + lax.rem(xx, 2))

    yp, ym, yo = lax.rem(y + 1, 4), lax.rem(y + 3, 4), lax.rem(y + 2, 4)
    xp, xm = lax.rem(x + 1, 4), lax.rem(x + 3, 4)
    zp, zm, zo = lax.rem(z + 1, 4), lax.rem(z + 3, 4), lax.rem(z + 2, 4)
    hp, hm = lax.div(xp, 2), lax.div(xm, 2)
    to_yp, to_ym = at(yp, z, x), at(ym, z, x)
    to_xp, to_xm = at(y, z, xp), at(y, z, xm)
    to_zp, to_zm, to_zo = at(y, zp, x), at(y, zm, x), at(y, zo, x)
    to_xl = (rep, d, 2 * z + 1 - xl)
    to_core = (1 - rep, d, t)

    count = [0]

    def remote(src, dst, target):
        k = count[0]
        count[0] += 1
        copy = pltpu.make_async_remote_copy(
            src_ref=src, dst_ref=dst, send_sem=send_sem.at[k], recv_sem=recv_sem.at[k],
            device_id=target, device_id_type=MESH,
        )
        copy.start()
        copies.append(copy)
        return copy

    copies = []
    sent = set()

    def wait_sent(copy):
        if id(copy) not in sent:
            sent.add(id(copy))
            copy.wait_send()

    loads = []
    for k, (src, dst) in enumerate(((wg_hbm, wg), (wu_hbm, wu), (wd_hbm, wd))):
        load = pltpu.make_async_copy(src, dst, local_sem.at[k])
        load.start()
        loads.append(load)

    def rows_of(start, size, step=16):
        return pl.ds(pl.multiple_of(start, step), size)

    own_rows = rows_of(t * OWN, OWN, OWN)
    mate_rows = rows_of((2 * z + 1 - xl) * OWN, OWN, OWN)
    tc_all[0, own_rows, :] = tok_in[...]
    tc_all[1, own_rows, :] = cot_in[...]

    barrier = pltpu.get_barrier_semaphore()
    peers = (to_yp, to_ym, to_xp, to_xm, to_zp, to_zm, to_zo, to_core)
    for peer in peers:
        pl.semaphore_signal(barrier, inc=1, device_id=peer, device_id_type=MESH)
    pl.semaphore_wait(barrier, len(peers))

    mate = remote(tc_all.at[:, own_rows], tc_all.at[:, own_rows], to_xl)
    gathers = [[], [], []]
    for k, target in enumerate((to_zp, to_zm, to_zo)):
        gathers[k].append(remote(tc_all.at[:, own_rows], tc_all.at[:, own_rows], target))
    frag_copy = remote(frag_in, frag_out, to_core)
    for load in loads:
        load.wait()

    live = [dict() for _ in range(CHUNKS)]

    def row0(c):
        return lax.rem(z + Z_ORDER[c], 4) * TC

    def stage_a(c):
        s, r0, me = c % SLOTS, row0(c), live[c]
        if c == 0:
            mate.wait_recv()
            for k, target in enumerate((to_zp, to_zm, to_zo)):
                gathers[k].append(remote(tc_all.at[:, mate_rows], tc_all.at[:, mate_rows], target))
        else:
            for copy in gathers[c - 1]:
                copy.wait_recv()
        if c >= SLOTS:
            for copy in live[c - SLOTS]["part_sends"]:
                wait_sent(copy)
        rows = rows_of(r0, TC, TC)

        def tile(k, carry):
            cols = pl.ds(pl.multiple_of(k * TILE, TILE), TILE)
            tok, cot = tc_all[0, rows, :], tc_all[1, rows, :]
            part[s, 0, :, cols] = dot(tok, wg[:, cols]).astype(BF16)
            part[s, 1, :, cols] = dot(tok, wu[:, cols]).astype(BF16)
            part[s, 2, :, cols] = dot(cot, wd[cols, :], 1, 1).astype(BF16)
            return carry

        lax.fori_loop(0, CY // TILE, tile, 0)
        ps = part.at[s]
        opp, up_b, down_b = rows_of(yo * YB, YB), rows_of(yp * YB, YB), rows_of(ym * YB, YB)
        me["s1"] = [
            remote(ps.at[:, opp, pl.ds(0, HY)], ra.at[c, 0], to_yp),
            remote(ps.at[:, opp, pl.ds(HY, HY)], ra.at[c, 1], to_ym),
            remote(ps.at[:, up_b, pl.ds(HY, HY)], rb.at[c, 0, :, :, pl.ds(HY, HY)], to_yp),
            remote(ps.at[:, down_b, pl.ds(0, HY)], rb.at[c, 1, :, :, pl.ds(0, HY)], to_ym),
        ]
        lax.fori_loop(CY // TILE, UNITS // TILE, tile, 0)
        me["t1"] = [
            remote(ps.at[:, rows_of(hp * XR, XR), pl.ds(CY, CX)], xa.at[c, 0], to_xp),
            remote(ps.at[:, rows_of(hm * XR, XR), pl.ds(CY, CX)], xa.at[c, 1], to_xm),
        ]
        me["part_sends"] = me["s1"] + me["t1"]
        for k in range(2):
            tc_t[k, :, rows] = tc_all[k, rows, :].T

    def stage_by(c):
        s, me = c % SLOTS, live[c]
        ps = part.at[s]
        me["s2"] = []
        for k, (blk, target) in enumerate(((yp, to_yp), (ym, to_ym))):
            rows, cols = rows_of(blk * YB, YB), pl.ds(k * HY, HY)
            me["s1"][k].wait_recv()
            for a in range(3):
                part[s, a, rows, cols] = (part[s, a, rows, cols].astype(F32) + ra[c, k, a].astype(F32)).astype(BF16)
            me["s2"].append(remote(ps.at[:, rows, cols], rb.at[c, k, :, :, cols], target))
        me["part_sends"] += me["s2"]

    def stage_bx(c):
        me = live[c]
        for copy in me["t1"]:
            copy.wait_recv()
        for blk in (yo, yp, ym):
            rows = rows_of(blk * XB, XB)
            for a in range(3):
                xa[c, 0, a, rows, :] = (xa[c, 0, a, rows, :].astype(F32) + xa[c, 1, a, rows, :].astype(F32)).astype(BF16)
            if blk is yo:
                me["t2"] = [
                    remote(xa.at[c, 0, :, rows, pl.ds(0, HX)], xb.at[c, 0], to_yp),
                    remote(xa.at[c, 0, :, rows, pl.ds(HX, HX)], xb.at[c, 1], to_ym),
                ]
        me["t3"] = [
            remote(xa.at[c, 0, :, rows_of(yp * XB, XB), pl.ds(HX, HX)], xc.at[c, 0, :, :, pl.ds(HX, HX)], to_yp),
            remote(xa.at[c, 0, :, rows_of(ym * XB, XB), pl.ds(0, HX)], xc.at[c, 1, :, :, pl.ds(0, HX)], to_ym),
        ]

    def stage_cy(c):
        s, me = c % SLOTS, live[c]
        for copy in me["s1"][2:] + me["s2"]:
            copy.wait_recv()
        rows = rows_of(y * YB, YB)
        for h in range(2):
            cols = pl.ds(h * HY, HY)
            for a in range(3):
                total = part[s, a, rows, cols].astype(F32) + rb[c, 0, a, :, cols].astype(F32)
                sy[c, h, a] = (total + rb[c, 1, a, :, cols].astype(F32)).astype(BF16)
        me["s3"] = [
            remote(sy.at[c, hp], rc.at[c, 0], to_xp),
            remote(sy.at[c, hm], rc.at[c, 1], to_xm),
        ]

    def stage_cx(c):
        me = live[c]
        for k, (blk, target) in enumerate(((yp, to_yp), (ym, to_ym))):
            rows, cols = rows_of(blk * XB, XB), pl.ds(k * HX, HX)
            me["t2"][k].wait_recv()
            for a in range(3):
                xa[c, 0, a, rows, cols] = (xa[c, 0, a, rows, cols].astype(F32) + xb[c, k, a].astype(F32)).astype(BF16)
            me["t3"].append(remote(xa.at[c, 0, :, rows, cols], xc.at[c, k, :, :, cols], target))

    def stage_dy(c):
        me = live[c]
        for copy in me["s3"]:
            copy.wait_recv()
        sums = [rc[c, 0, a].astype(F32) + rc[c, 1, a].astype(F32) for a in range(3)]
        for a, value in enumerate(pointwise(*sums)):
            e_own[c, a] = value
        place = h_all.at[:, rows_of(row0(c) + y * YB, YB), pl.ds(pl.multiple_of(xh * HY, HY), HY)]
        me["s4"] = [remote(e_own.at[c], place, target) for target in (to_xp, to_xm)]

    def stage_dx(c):
        me = live[c]
        for copy in me["t3"]:
            copy.wait_recv()
        rows = rows_of(y * XB, XB)
        sums = []
        for a in range(3):
            total = xa[c, 0, a, rows, :].astype(F32) + xa[c, 1, a, rows, :].astype(F32)
            sums.append(total + (xc[c, 0, a].astype(F32) + xc[c, 1, a].astype(F32)))
        for a, value in enumerate(pointwise(*sums)):
            g_all[c, a, rows, :] = value
        place = g_all.at[c, :, rows]
        me["t4"] = [remote(place, place, target) for target in (to_yp, to_ym)]

    def stage_ey(c):
        me = live[c]
        for copy in me["s4"]:
            copy.wait_recv()
        place = h_all.at[:, rows_of(row0(c) + y * YB, YB), pl.ds(0, CY)]
        me["s5"] = [remote(place, place, target) for target in (to_yp, to_ym)]

    def stage_ex(c):
        me = live[c]
        me["t5"] = []
        for k, (blk, target) in enumerate(((ym, to_yp), (yp, to_ym))):
            me["t4"][k].wait_recv()
            place = g_all.at[c, :, rows_of(blk * XB, XB), pl.ds(k * HX, HX)]
            me["t5"].append(remote(place, place, target))

    def stage_fy(c):
        me = live[c]
        me["s6"] = []
        for k, (blk, target) in enumerate(((ym, to_yp), (yp, to_ym))):
            me["s5"][k].wait_recv()
            place = h_all.at[:, rows_of(row0(c) + blk * YB, YB), pl.ds(k * HY, HY)]
            me["s6"].append(remote(place, place, target))

    def stage_fx(c):
        me = live[c]
        for copy in me["t5"]:
            copy.wait_recv()
        place = h_all.at[:, rows_of(row0(c) + xh * XR, XR), pl.ds(CY, CX)]
        me["t6"] = [remote(g_all.at[c], place, target) for target in (to_xp, to_xm)]

    zsum = []

    def stage_g(c):
        me = live[c]
        for copy in me["s6"] + me["t6"]:
            copy.wait_recv()
        rows = rows_of(row0(c), TC, TC)

        def tile(k, carry):
            cols = pl.ds(pl.multiple_of(k * TILE, TILE), TILE)
            ms[c, 0, :, cols] = dot(h_all[0, rows, :], wd[:, cols]).astype(BF16)
            term = dot(h_all[1, rows, :], wg[cols, :], 1, 1) + dot(h_all[2, rows, :], wu[cols, :], 1, 1)
            ms[c, 1, :, cols] = term.astype(BF16)
            return carry

        lax.fori_loop(0, DIM // TILE, tile, 0)
        if c:
            zsum.append(remote(ms.at[c], rz.at[c - 1], (to_zm, to_zp, to_zo)[c - 1]))

    stages = dict(
        A=stage_a, By=stage_by, Bx=stage_bx, Cy=stage_cy, Cx=stage_cx, Dy=stage_dy, Dx=stage_dx,
        Ey=stage_ey, Ex=stage_ex, Fy=stage_fy, Fx=stage_fx, G=stage_g,
    )
    for name, c in tick_order():
        stages[name](c)

    def grad_tile(k, carry):
        cols = pl.ds(pl.multiple_of(k * TILE, TILE), TILE)
        gg[:, cols] = dot(tc_t[0], h_all[1, :, cols]).astype(BF16)
        ug[:, cols] = dot(tc_t[0], h_all[2, :, cols]).astype(BF16)
        dg[cols, :] = dot(tc_t[1], h_all[0, :, cols]).astype(BF16).T
        return carry

    lax.fori_loop(0, UNITS // TILE, grad_tile, 0)
    stores = []
    for k, (src, dst) in enumerate(((gg, gg_out), (ug, ug_out), (dg, dg_out))):
        store = pltpu.make_async_copy(src, dst, local_sem.at[3 + k])
        store.start()
        stores.append(store)

    for copy in zsum:
        copy.wait_recv()
    mine, theirs = rows_of(xl * OWN, OWN, OWN), rows_of((1 - xl) * OWN, OWN, OWN)

    def zsum_of(k, rows):
        total = ms[0, k, rows, :].astype(F32)
        for j in range(3):
            total = total + rz[j, k, rows, :].astype(F32)
        return total

    for k in range(2):
        ms[0, k, theirs, :] = zsum_of(k, theirs).astype(BF16)
    last = remote(ms.at[0, :, theirs], rx, to_xl)
    totals = [zsum_of(k, mine) for k in range(2)]
    last.wait_recv()
    mixed_out[...] = (totals[0] + rx[0].astype(F32)).astype(BF16)
    ig_out[...] = (totals[1] + rx[1].astype(F32)).astype(BF16)
    frag_copy.wait_recv()
    for copy in copies:
        wait_sent(copy)
    for store in stores:
        store.wait()


def shards(tokens, cotangent, gate_weight, up_weight, down_weight, frag_delta, outer_momentum):
    vmem, anywhere = pl.BlockSpec(memory_space=pltpu.VMEM), pl.BlockSpec(memory_space=pl.ANY)
    side = jax.ShapeDtypeStruct((OWN, DIM), BF16)
    wide = jax.ShapeDtypeStruct((DIM, UNITS), BF16)
    tall = jax.ShapeDtypeStruct((UNITS, DIM), BF16)
    mixed, input_grad, gate_grad, up_grad, down_grad, other = pl.pallas_call(
        kernel,
        out_shape=(side, side, wide, wide, tall, tall),
        in_specs=[vmem, vmem] + [anywhere] * 4,
        out_specs=(vmem, vmem, anywhere, anywhere, anywhere, anywhere),
        scratch_shapes=[
            pltpu.VMEM((DIM, UNITS), BF16),
            pltpu.VMEM((DIM, UNITS), BF16),
            pltpu.VMEM((UNITS, DIM), BF16),
            pltpu.VMEM((2, ROWS, DIM), BF16),
            pltpu.VMEM((2, DIM, ROWS), BF16),
            pltpu.VMEM((SLOTS, 3, TC, UNITS), BF16),
            pltpu.VMEM((3, ROWS, UNITS), BF16),
            pltpu.VMEM((CHUNKS, 2, 3, YB, HY), BF16),
            pltpu.VMEM((CHUNKS, 2, 3, YB, CY), BF16),
            pltpu.VMEM((CHUNKS, 2, 3, YB, HY), BF16),
            pltpu.VMEM((CHUNKS, 2, 3, YB, HY), BF16),
            pltpu.VMEM((CHUNKS, 3, YB, HY), BF16),
            pltpu.VMEM((CHUNKS, 2, 3, XR, CX), BF16),
            pltpu.VMEM((CHUNKS, 2, 3, XB, HX), BF16),
            pltpu.VMEM((CHUNKS, 2, 3, XB, CX), BF16),
            pltpu.VMEM((CHUNKS, 3, XR, CX), BF16),
            pltpu.VMEM((CHUNKS, 2, TC, DIM), BF16),
            pltpu.VMEM((3, 2, TC, DIM), BF16),
            pltpu.VMEM((2, OWN, DIM), BF16),
            pltpu.VMEM((DIM, UNITS), BF16),
            pltpu.VMEM((DIM, UNITS), BF16),
            pltpu.VMEM((UNITS, DIM), BF16),
            pltpu.SemaphoreType.DMA((SEMS,)),
            pltpu.SemaphoreType.DMA((SEMS,)),
            pltpu.SemaphoreType.DMA((6,)),
        ],
        compiler_params=pltpu.CompilerParams(
            collective_id=0, has_side_effects=True, vmem_limit_bytes=60 * 1024 * 1024
        ),
        cost_estimate=pl.CostEstimate(flops=18 * ROWS * DIM * UNITS, bytes_accessed=16_000_000, transcendentals=0),
        name="layer",
    )(tokens[0], cotangent[0], gate_weight[0], up_weight[0], down_weight[0], frag_delta[0])
    mean_delta = (frag_delta[0].astype(F32) + other.astype(F32)) / lax.axis_size("replica")
    momentum_next = momentum_rate * outer_momentum + mean_delta
    outer_step = outer_rate * (mean_delta + momentum_rate * momentum_next)
    return (
        mixed[None], input_grad[None], gate_grad[None], up_grad[None], down_grad[None],
        outer_step, momentum_next,
    )


def solution(mesh):
    act, wide, tall = P("replica", "tensor", "dp"), P("replica", "dp", "tensor"), P("replica", "tensor", "dp")
    state = P("tensor", "dp")
    return jax.shard_map(
        shards,
        mesh=mesh,
        in_specs=(act, act, wide, wide, tall, tall, state),
        out_specs=(act, act, wide, wide, tall, state, state),
        check_vma=False,
    )
```

time: 666 us -> 203 us (0.30)
  waiting for transfers between devices: 590 us -> 0 us
  Pallas kernels: 0 us -> 188 us
  matrix products: 38.1 us -> 0 us
  between operations: 14.2 us -> 0.69 us
  other arithmetic: 15.3 us -> 6.42 us
    psum x2 -> x0, waiting for transfers between devices: 449 us -> none  [the longest x1 440 us: shards(): lax.psum(up_part.astype(jnp.bfloat16), 'dp').astype(jnp.float32)]
    pallas_call x0 -> x1, Pallas kernels: none -> 188 us  [shards(): pl.pallas_call(kernel, out_shape=(side, side, wide, wide, tall, tall), in...]
    all_gather x2 -> x0, waiting for transfers between devices: 76.5 us -> none  [the longest x1 44 us: shards(): lax.all_gather(tokens[0], 'tensor', axis=0, tiled=True)]
    reduce_scatter x2 -> x0, waiting for transfers between devices: 62.4 us -> none  [the longest x1 43 us: shards(): lax.psum_scatter(jnp.dot(hidden, w_down, preferred_element_type=jnp.float...]
    dot_general x9 -> x0, matrix products: 38.1 us -> none  [the longest x1 5.69 us: shards(): jnp.einsum('td,fd->tf', slopes_all, w_down, preferred_element_type=jnp.fl...]
    convert_element_type x1 -> x0, other arithmetic: 8.32 us -> none  [shards(): (hidden_grad * up * sigma * (1.0 + gate * (1.0 - sigma))).astype(jnp.bflo...]
  transfers between devices with their start and end apart: 6 -> 0, of which waited for: 6 -> 0; matrix products, arithmetic and copies ran while one was open for 8% -> 0% of each run, Pallas kernels for 0% -> 0%
where the time goes in v1:
time: 203 us; the launch traced here: 200 us
  Pallas kernels  188 us (93%)
  other arithmetic  6.42 us (3%)
  local copies, waits for them, and re-layouts  5.02 us (2%)
    pallas_call x1, Pallas kernels, shards(): pl.pallas_call(kernel, out_shape=(side, side, wide, wide, tall, tall), in...  188 us
    mul x1, other arithmetic, shards(): outer_step = outer_rate * (mean_delta + momentum_rate * momentum_next)  6.42 us
    unnamed x17, local copies, waits for them, and re-layouts  5.02 us

profile of v1, /device:TPU:0, one launch (start us, length us, event | category | flops | bytes accessed | tf_op | source)
XLA Modules:
  0.0 200.5 jit_solution(8519055761419977504)
XLA Ops:
  0.6 0.0 copy-start
  0.6 188.4 %layer.1 = (bf16[128,512]{1,0:T(8,128)(2,1)}, bf16[128,512]{1,0:T(8,128)(2,1)}, bf16[512,1792]{1,0:T(8,128)(2,1)}, bf16[512,1792]{1,0:T(8,128)(2,1)}, bf16[1792,...) custom-call(bf16[128,512]{1,0:T(8,128)(2,1)} %bitcast.23, bf16[128,512]{1,0:T(8,128)(2,1)} %bitcast.24, ...), custom_call_target="tpu_custom_call" | custom-call | flops 16911433728 | bytes 16000000 | tf_op jit(solution)/shard_map/layer/pallas_call | solution.py:367
  189.0 0.0 copy-done
  189.0 0.0 copy-start.5
  189.0 0.0 copy-start.4
  189.0 0.0 copy-start.3
  189.1 6.4 %add_multiply_fusion = (f32[1792,512]{1,0:T(8,128)}, f32[1792,512]{1,0:T(8,128)}) fusion(bf16[1792,512]{1,0:T(8,128)(2,1)} %get-tuple-element.18, bf16[1,1792,512]{2,1,0:T(8,128)(2,1)} %param.12, f32[1792,512]{1,0:T(8,128)S(1)} %copy-done), kind=kLoop, calls=%fused_computation | loop fusion | flops 8257536 | bytes 14680064 | tf_op jit(solution)/shard_map/mul | solution.py:407
  195.5 0.0 copy-start.2
  195.5 0.0 copy-done.5
  195.5 0.7 copy.19
  196.1 0.0 copy-done.4
  196.1 0.7 copy.20
  196.8 0.0 copy-done.3
  196.8 0.0 copy-start.1
  196.8 1.2 copy.21
  198.0 0.0 copy-done.2
  198.0 1.2 copy.22
  199.3 0.0 copy-done.1
  199.3 1.2 copy.23
Async XLA Ops:
  0.6 188.4 %copy-start = (f32[1792,512]{1,0:T(8,128)S(1)}, f32[1792,512]{1,0:T(8,128)}, u32[]{:S(2)}) copy-start(f32[1792,512]{1,0:T(8,128)} %param.13) | copy-start | bytes 11010052
  189.0 6.5 %copy-start.5 = (bf16[128,512]{1,0:T(8,128)(2,1)S(1)}, bf16[128,512]{1,0:T(8,128)(2,1)}, u32[]{:S(2)}) copy-start(bf16[128,512]{1,0:T(8,128)(2,1)} %get-tuple-element.13) | copy-start | bytes 393220
  189.0 7.1 %copy-start.4 = (bf16[128,512]{1,0:T(8,128)(2,1)S(1)}, bf16[128,512]{1,0:T(8,128)(2,1)}, u32[]{:S(2)}) copy-start(bf16[128,512]{1,0:T(8,128)(2,1)} %get-tuple-element.14) | copy-start | bytes 393220
  189.0 7.8 %copy-start.3 = (bf16[512,1792]{1,0:T(8,128)(2,1)S(1)}, bf16[512,1792]{1,0:T(8,128)(2,1)}, u32[]{:S(2)}) copy-start(bf16[512,1792]{1,0:T(8,128)(2,1)} %get-tuple-element.15) | copy-start | bytes 5505028
  195.5 2.6 %copy-start.2 = (bf16[512,1792]{1,0:T(8,128)(2,1)S(1)}, bf16[512,1792]{1,0:T(8,128)(2,1)}, u32[]{:S(2)}) copy-start(bf16[512,1792]{1,0:T(8,128)(2,1)} %get-tuple-element.16) | copy-start | bytes 5505028
  196.8 2.5 %copy-start.1 = (bf16[1792,512]{1,0:T(8,128)(2,1)S(1)}, bf16[1792,512]{1,0:T(8,128)(2,1)}, u32[]{:S(2)}) copy-start(bf16[1792,512]{1,0:T(8,128)(2,1)} %get-tuple-element.17) | copy-start | bytes 5505028

commit v2 on v1

v2 whole, which is shorter than its diff:
```python
import functools

import jax
import jax.numpy as jnp
from jax import lax
from jax.experimental import pallas as pl
from jax.experimental.pallas import tpu as pltpu
from jax.sharding import PartitionSpec as P

MESH = pl.DeviceIdType.MESH
F32 = jnp.float32
BF16 = jnp.bfloat16
momentum_rate = 0.9
outer_rate = 0.7

ROWS = 1024
OWN = 128
DIM = 512
UNITS = 1792
SIZES = (128, 256, 256, 256, 128)
STARTS = (0, 128, 384, 640, 896)
CHUNKS = len(SIZES)
SLOTS = 2
CY = 1024
CX = UNITS - CY
HY = CY // 2
HX = CX // 2
TILE = 256
SEMS = 224

ORDER = (
    "A0", "By0", "Bx0", "Bz0", "M0", "Cy0", "Cx0", "Dx0", "Dy0", "A1", "Ex0", "Ey0", "A2", "By1", "Bx1", "Fx0",
    "Bz1", "Fy0", "By2", "Bx2", "Cy1", "Bz2", "Cx1", "A3", "G0", "Dy1", "Cy2", "Cx2", "A4", "Bx3", "Dx1", "By3",
    "Bz3", "Dx2", "Ey1", "By4", "Cx3", "Dy2", "Bx4", "Ex1", "Bz4", "Cy3", "Ex2", "Ey2", "Fy1", "Cy4", "Dx3", "Cx4",
    "Fx1", "Dy3", "Fx2", "Dy4", "Fy2", "G1", "Ex3", "Dx4", "Ey3", "G2", "Fx3", "Ey4", "Ex4", "Fy3", "Fy4", "Fx4",
    "G3", "G4",
)


def pointwise(gate, up, hidden_grad):
    sigma = jax.nn.sigmoid(gate)
    active = gate * sigma
    hidden = active * up
    gate_slope = hidden_grad * up * sigma * (1.0 + gate * (1.0 - sigma))
    up_slope = hidden_grad * active
    return hidden.astype(BF16), gate_slope.astype(BF16), up_slope.astype(BF16)


def dot(a, b, ca=1, cb=0):
    return lax.dot_general(a, b, (((ca,), (cb,)), ((), ())), preferred_element_type=F32)


def kernel(
    tok_in, cot_in, wg_hbm, wu_hbm, wd_hbm, frag_in,
    mixed_out, ig_out, gg_out, ug_out, dg_out, frag_out,
    wg, wu, wd, tc_all, tc_t, part, h_all, ra, rb, sy, rc, e_own, xa, xb, xc, g_all, ms, ml, own, rz, rx, gg, ug, dg,
    send_sem, recv_sem, local_sem,
):
    rep, d, t = lax.axis_index("replica"), lax.axis_index("dp"), lax.axis_index("tensor")
    y, xh = lax.div(d, 2), lax.rem(d, 2)
    z, xl = lax.div(t, 2), lax.rem(t, 2)
    x = 2 * xh + xl

    def at(yy, zz, xx):
        return (rep, yy * 2 + lax.div(xx, 2), zz * 2 + lax.rem(xx, 2))

    yp, ym, yo = lax.rem(y + 1, 4), lax.rem(y + 3, 4), lax.rem(y + 2, 4)
    xp, xm = lax.rem(x + 1, 4), lax.rem(x + 3, 4)
    zp, zm, zo = lax.rem(z + 1, 4), lax.rem(z + 3, 4), lax.rem(z + 2, 4)
    hp, hm = lax.div(xp, 2), lax.div(xm, 2)
    to_yp, to_ym = at(yp, z, x), at(ym, z, x)
    to_xp, to_xm = at(y, z, xp), at(y, z, xm)
    to_zp, to_zm, to_zo = at(y, zp, x), at(y, zm, x), at(y, zo, x)
    to_xl = (rep, d, 2 * z + 1 - xl)
    to_core = (1 - rep, d, t)

    count = [0]

    def remote(src, dst, target):
        k = count[0]
        count[0] += 1
        copy = pltpu.make_async_remote_copy(
            src_ref=src, dst_ref=dst, send_sem=send_sem.at[k], recv_sem=recv_sem.at[k],
            device_id=target, device_id_type=MESH,
        )
        copy.start()
        copies.append(copy)
        return copy

    copies = []
    sent = set()

    def wait_sent(copy):
        if id(copy) not in sent:
            sent.add(id(copy))
            copy.wait_send()

    loads = []
    for k, (src, dst) in enumerate(((wg_hbm, wg), (wu_hbm, wu), (wd_hbm, wd))):
        load = pltpu.make_async_copy(src, dst, local_sem.at[k])
        load.start()
        loads.append(load)

    def rows_of(start, size, step=16):
        return pl.ds(pl.multiple_of(start, step), size)

    own_rows = rows_of(t * OWN, OWN, OWN)
    mate_rows = rows_of((2 * z + 1 - xl) * OWN, OWN, OWN)
    tc_all[0, own_rows, :] = tok_in[...]
    tc_all[1, own_rows, :] = cot_in[...]

    barrier = pltpu.get_barrier_semaphore()
    peers = (to_yp, to_ym, to_xp, to_xm, to_zp, to_zm, to_zo, to_core)
    for peer in peers:
        pl.semaphore_signal(barrier, inc=1, device_id=peer, device_id_type=MESH)
    pl.semaphore_wait(barrier, len(peers))

    mate = remote(tc_all.at[:, own_rows], tc_all.at[:, own_rows], to_xl)
    z_targets = (to_zp, to_zm, to_zo)
    gathers = [[remote(tc_all.at[:, own_rows], tc_all.at[:, own_rows], target)] for target in z_targets]
    frag_copy = remote(frag_in, frag_out, to_core)
    for load in loads:
        load.wait()

    live = [dict() for _ in range(CHUNKS)]

    def row0(c, side):
        if c in (1, 2, 3):
            return (zm, zp, zo)[c - 1] * 2 * OWN
        return (2 * z + (side if c == 0 else 1 - side)) * OWN

    def y_rows(c, blk, base=0):
        return rows_of(base + blk * (SIZES[c] // 4), SIZES[c] // 4)

    def x_rows(c, blk, base=0):
        return rows_of(base + blk * (SIZES[c] // 8), SIZES[c] // 8)

    def y_own(c):
        return pl.ds(STARTS[c] // 4, SIZES[c] // 4)

    def x_own(c):
        return pl.ds(STARTS[c] // 8, SIZES[c] // 8)

    def xa_rows(c, blk):
        return x_rows(c, blk, STARTS[c] // 2)

    def stage_m(c):
        mate.wait_recv()
        for k, target in enumerate(z_targets):
            gathers[k].append(remote(tc_all.at[:, mate_rows], tc_all.at[:, mate_rows], target))

    def stage_a(c):
        s, size, me = c % SLOTS, SIZES[c], live[c]
        if c in (1, 2, 3):
            for copy in gathers[c - 1]:
                copy.wait_recv()
        if c >= SLOTS:
            for copy in live[c - SLOTS]["part_sends"]:
                wait_sent(copy)
        rows = rows_of(row0(c, xl), size, OWN)
        kept = pl.ds(0, size)

        def tile(k, carry):
            cols = pl.ds(pl.multiple_of(k * TILE, TILE), TILE)
            tok, cot = tc_all[0, rows, :], tc_all[1, rows, :]
            part[s, 0, kept, cols] = dot(tok, wg[:, cols]).astype(BF16)
            part[s, 1, kept, cols] = dot(tok, wu[:, cols]).astype(BF16)
            part[s, 2, kept, cols] = dot(cot, wd[cols, :], 1, 1).astype(BF16)
            return carry

        lax.fori_loop(0, CY // TILE, tile, 0)
        ps = part.at[s]
        first, second = pl.ds(0, HY), pl.ds(HY, HY)
        me["s1"] = [
            remote(ps.at[:, y_rows(c, yo), first], ra.at[0, :, y_own(c)], to_yp),
            remote(ps.at[:, y_rows(c, yo), second], ra.at[1, :, y_own(c)], to_ym),
            remote(ps.at[:, y_rows(c, yp), second], rb.at[0, :, y_own(c), second], to_yp),
            remote(ps.at[:, y_rows(c, ym), first], rb.at[1, :, y_own(c), first], to_ym),
        ]
        lax.fori_loop(CY // TILE, UNITS // TILE, tile, 0)
        me["t1"] = []
        for blk in (yo, yp, ym, y):
            for k, (half, target) in enumerate(((hp, to_xp), (hm, to_xm))):
                src = ps.at[:, x_rows(c, blk, half * (size // 2)), pl.ds(CY, CX)]
                me["t1"].append(remote(src, xa.at[k, :, xa_rows(c, blk)], target))
        me["part_sends"] = me["s1"] + me["t1"]
        for k in range(2):
            tc_t[k, :, rows] = tc_all[k, rows, :].T

    def stage_by(c):
        s, me = c % SLOTS, live[c]
        me["s2"] = []
        for k, (blk, target) in enumerate(((yp, to_yp), (ym, to_ym))):
            rows, cols = y_rows(c, blk), pl.ds(k * HY, HY)
            me["s1"][k].wait_recv()
            for a in range(3):
                total = part[s, a, rows, cols].astype(F32) + ra[k, a, y_own(c), :].astype(F32)
                part[s, a, rows, cols] = total.astype(BF16)
            me["s2"].append(remote(part.at[s, :, rows, cols], rb.at[k, :, y_own(c), cols], target))
        me["part_sends"] += me["s2"]

    def add_sides(c, blk):
        rows = xa_rows(c, blk)
        for a in range(3):
            xa[0, a, rows, :] = (xa[0, a, rows, :].astype(F32) + xa[1, a, rows, :].astype(F32)).astype(BF16)

    def stage_bx(c):
        me = live[c]
        for copy in me["t1"][:2]:
            copy.wait_recv()
        add_sides(c, yo)
        rows = xa_rows(c, yo)
        me["t2"] = [
            remote(xa.at[0, :, rows, pl.ds(0, HX)], xb.at[0, :, x_own(c)], to_yp),
            remote(xa.at[0, :, rows, pl.ds(HX, HX)], xb.at[1, :, x_own(c)], to_ym),
        ]

    def stage_bz(c):
        me = live[c]
        for copy in me["t1"][2:6]:
            copy.wait_recv()
        me["t3"] = []
        for k, (blk, target) in enumerate(((yp, to_yp), (ym, to_ym))):
            add_sides(c, blk)
            cols = pl.ds((1 - k) * HX, HX)
            me["t3"].append(remote(xa.at[0, :, xa_rows(c, blk), cols], xc.at[k, :, x_own(c), cols], target))

    def stage_cy(c):
        s, me = c % SLOTS, live[c]
        for copy in me["s1"][2:] + me["s2"]:
            copy.wait_recv()
        rows, own = y_rows(c, y), y_own(c)
        for h in range(2):
            cols = pl.ds(h * HY, HY)
            for a in range(3):
                total = part[s, a, rows, cols].astype(F32) + rb[0, a, own, cols].astype(F32)
                sy[h, a, own, :] = (total + rb[1, a, own, cols].astype(F32)).astype(BF16)
        me["s3"] = [
            remote(sy.at[half, :, own], rc.at[k, :, own], target)
            for k, (half, target) in enumerate(((hp, to_xp), (hm, to_xm)))
        ]

    def stage_cx(c):
        me = live[c]
        for k, (blk, target) in enumerate(((yp, to_yp), (ym, to_ym))):
            rows, cols = xa_rows(c, blk), pl.ds(k * HX, HX)
            me["t2"][k].wait_recv()
            for a in range(3):
                total = xa[0, a, rows, cols].astype(F32) + xb[k, a, x_own(c), :].astype(F32)
                xa[0, a, rows, cols] = total.astype(BF16)
            me["t3"].append(remote(xa.at[0, :, rows, cols], xc.at[k, :, x_own(c), cols], target))

    def stage_dy(c):
        me, own = live[c], y_own(c)
        for copy in me["s3"]:
            copy.wait_recv()
        sums = [rc[0, a, own, :].astype(F32) + rc[1, a, own, :].astype(F32) for a in range(3)]
        for a, value in enumerate(pointwise(*sums)):
            e_own[a, own, :] = value
        place = h_all.at[:, y_rows(c, y, row0(c, 1 - xl)), pl.ds(pl.multiple_of(xh * HY, HY), HY)]
        me["s4"] = [remote(e_own.at[:, own], place, target) for target in (to_xp, to_xm)]

    def send_x(c, blk):
        place = h_all.at[:, x_rows(c, blk, row0(c, 1 - xl) + xh * (SIZES[c] // 2)), pl.ds(CY, CX)]
        live[c]["t6"] += [remote(g_all.at[:, xa_rows(c, blk)], place, target) for target in (to_xp, to_xm)]

    def stage_dx(c):
        me, own = live[c], x_own(c)
        for copy in me["t3"] + me["t1"][6:]:
            copy.wait_recv()
        rows = xa_rows(c, y)
        sums = []
        for a in range(3):
            total = xa[0, a, rows, :].astype(F32) + xa[1, a, rows, :].astype(F32)
            sums.append(total + (xc[0, a, own, :].astype(F32) + xc[1, a, own, :].astype(F32)))
        for a, value in enumerate(pointwise(*sums)):
            g_all[a, rows, :] = value
        place = g_all.at[:, rows]
        me["t4"] = [remote(place, place, target) for target in (to_yp, to_ym)]
        me["t6"] = []
        send_x(c, y)

    def stage_ey(c):
        me = live[c]
        for copy in me["s4"]:
            copy.wait_recv()
        place = h_all.at[:, y_rows(c, y, row0(c, xl)), pl.ds(0, CY)]
        me["s5"] = [remote(place, place, target) for target in (to_yp, to_ym)]

    def stage_ex(c):
        me = live[c]
        me["t5"] = []
        for k, (blk, target) in enumerate(((ym, to_yp), (yp, to_ym))):
            me["t4"][k].wait_recv()
            place = g_all.at[:, xa_rows(c, blk), pl.ds(k * HX, HX)]
            me["t5"].append(remote(place, place, target))
        for blk in (ym, yp):
            send_x(c, blk)

    def stage_fy(c):
        me = live[c]
        me["s6"] = []
        for k, (blk, target) in enumerate(((ym, to_yp), (yp, to_ym))):
            me["s5"][k].wait_recv()
            place = h_all.at[:, y_rows(c, blk, row0(c, xl)), pl.ds(k * HY, HY)]
            me["s6"].append(remote(place, place, target))

    def stage_fx(c):
        for copy in live[c]["t5"]:
            copy.wait_recv()
        send_x(c, yo)

    zsum = []
    last = []

    def stage_g(c):
        me = live[c]
        for copy in me["s6"] + me["t6"]:
            copy.wait_recv()
        rows = rows_of(row0(c, xl), SIZES[c], OWN)
        if c == 4:
            for copy in zsum:
                copy.wait_recv()

        def keep(k, cols, value):
            if c == 0:
                own[k, :, cols] = value
            elif c == 4:
                ml[k, :, cols] = (value + z_sum(k, 1 - xl, cols)).astype(BF16)
            else:
                ms[c - 1, k, :, cols] = value.astype(BF16)

        def mixed_tile(k, carry):
            cols = pl.ds(pl.multiple_of(k * TILE, TILE), TILE)
            keep(0, cols, dot(h_all[0, rows, :], wd[:, cols]))
            return carry

        def ig_tile(k, carry):
            cols = pl.ds(pl.multiple_of(k * TILE, TILE), TILE)
            term = dot(h_all[1, rows, :], wg[cols, :], 1, 1) + dot(h_all[2, rows, :], wu[cols, :], 1, 1)
            keep(1, cols, term)
            return carry

        for k, body in enumerate((mixed_tile, ig_tile)):
            lax.fori_loop(0, DIM // TILE, body, 0)
            if c == 4:
                last.append(remote(ml.at[k], rx.at[k], to_xl))
        if c in (1, 2, 3):
            zsum.append(remote(ms.at[c - 1], rz.at[c - 1], (to_zm, to_zp, to_zo)[c - 1]))

    def z_sum(k, side, cols):
        rows = rows_of(side * OWN, OWN, OWN)
        total = rz[0, k, rows, cols].astype(F32) + rz[1, k, rows, cols].astype(F32)
        return total + rz[2, k, rows, cols].astype(F32)

    stages = dict(
        A=stage_a, M=stage_m, By=stage_by, Bx=stage_bx, Bz=stage_bz, Cy=stage_cy, Cx=stage_cx, Dy=stage_dy,
        Dx=stage_dx, Ey=stage_ey, Ex=stage_ex, Fy=stage_fy, Fx=stage_fx, G=stage_g,
    )
    for step in ORDER:
        stages[step[:-1]](int(step[-1]))

    def grad_tile(k, carry):
        cols = pl.ds(pl.multiple_of(k * TILE, TILE), TILE)
        gg[:, cols] = dot(tc_t[0], h_all[1, :, cols]).astype(BF16)
        ug[:, cols] = dot(tc_t[0], h_all[2, :, cols]).astype(BF16)
        dg[cols, :] = dot(tc_t[1], h_all[0, :, cols]).astype(BF16).T
        return carry

    lax.fori_loop(0, UNITS // TILE, grad_tile, 0)
    stores = []
    for k, (src, dst) in enumerate(((gg, gg_out), (ug, ug_out), (dg, dg_out))):
        store = pltpu.make_async_copy(src, dst, local_sem.at[3 + k])
        store.start()
        stores.append(store)

    for k, out in enumerate((mixed_out, ig_out)):
        total = own[k] + z_sum(k, xl, pl.ds(0, DIM))
        last[k].wait_recv()
        out[...] = (total + rx[k].astype(F32)).astype(BF16)
    frag_copy.wait_recv()
    for copy in copies:
        wait_sent(copy)
    for store in stores:
        store.wait()


def shards(tokens, cotangent, gate_weight, up_weight, down_weight, frag_delta, outer_momentum):
    vmem, anywhere = pl.BlockSpec(memory_space=pltpu.VMEM), pl.BlockSpec(memory_space=pl.ANY)
    side = jax.ShapeDtypeStruct((OWN, DIM), BF16)
    wide = jax.ShapeDtypeStruct((DIM, UNITS), BF16)
    tall = jax.ShapeDtypeStruct((UNITS, DIM), BF16)
    mixed, input_grad, gate_grad, up_grad, down_grad, other = pl.pallas_call(
        kernel,
        out_shape=(side, side, wide, wide, tall, tall),
        in_specs=[vmem, vmem] + [anywhere] * 4,
        out_specs=(vmem, vmem, anywhere, anywhere, anywhere, anywhere),
        scratch_shapes=[
            pltpu.VMEM((DIM, UNITS), BF16),
            pltpu.VMEM((DIM, UNITS), BF16),
            pltpu.VMEM((UNITS, DIM), BF16),
            pltpu.VMEM((2, ROWS, DIM), BF16),
            pltpu.VMEM((2, DIM, ROWS), BF16),
            pltpu.VMEM((SLOTS, 3, max(SIZES), UNITS), BF16),
            pltpu.VMEM((3, ROWS, UNITS), BF16),
            pltpu.VMEM((2, 3, ROWS // 4, HY), BF16),
            pltpu.VMEM((2, 3, ROWS // 4, CY), BF16),
            pltpu.VMEM((2, 3, ROWS // 4, HY), BF16),
            pltpu.VMEM((2, 3, ROWS // 4, HY), BF16),
            pltpu.VMEM((3, ROWS // 4, HY), BF16),
            pltpu.VMEM((2, 3, ROWS // 2, CX), BF16),
            pltpu.VMEM((2, 3, ROWS // 8, HX), BF16),
            pltpu.VMEM((2, 3, ROWS // 8, CX), BF16),
            pltpu.VMEM((3, ROWS // 2, CX), BF16),
            pltpu.VMEM((3, 2, 2 * OWN, DIM), BF16),
            pltpu.VMEM((2, OWN, DIM), BF16),
            pltpu.VMEM((2, OWN, DIM), F32),
            pltpu.VMEM((3, 2, 2 * OWN, DIM), BF16),
            pltpu.VMEM((2, OWN, DIM), BF16),
            pltpu.VMEM((DIM, UNITS), BF16),
            pltpu.VMEM((DIM, UNITS), BF16),
            pltpu.VMEM((UNITS, DIM), BF16),
            pltpu.SemaphoreType.DMA((SEMS,)),
            pltpu.SemaphoreType.DMA((SEMS,)),
            pltpu.SemaphoreType.DMA((6,)),
        ],
        compiler_params=pltpu.CompilerParams(
            collective_id=0, has_side_effects=True, vmem_limit_bytes=60 * 1024 * 1024
        ),
        cost_estimate=pl.CostEstimate(flops=18 * ROWS * DIM * UNITS, bytes_accessed=16_000_000, transcendentals=0),
        name="layer",
    )(tokens[0], cotangent[0], gate_weight[0], up_weight[0], down_weight[0], frag_delta[0])
    mean_delta = (frag_delta[0].astype(F32) + other.astype(F32)) / lax.axis_size("replica")
    momentum_next = momentum_rate * outer_momentum + mean_delta
    outer_step = outer_rate * (mean_delta + momentum_rate * momentum_next)
    return (
        mixed[None], input_grad[None], gate_grad[None], up_grad[None], down_grad[None],
        outer_step, momentum_next,
    )


def solution(mesh):
    act, wide, tall = P("replica", "tensor", "dp"), P("replica", "dp", "tensor"), P("replica", "tensor", "dp")
    state = P("tensor", "dp")
    return jax.shard_map(
        shards,
        mesh=mesh,
        in_specs=(act, act, wide, wide, tall, tall, state),
        out_specs=(act, act, wide, wide, tall, state, state),
        check_vma=False,
    )
```

time: 203 us -> 196 us (0.966)
  Pallas kernels: 188 us -> 183 us
    pallas_call x1, Pallas kernels: 188 us -> 183 us  [shards(): pl.pallas_call(kernel, out_shape=(side, side, wide, wide, tall, tall), in...]
where the time goes in v2:
time: 196 us; the launch traced here: 195 us
  Pallas kernels  183 us (93%)
  other arithmetic  6.42 us (3%)
  local copies, waits for them, and re-layouts  5.02 us (3%)
    pallas_call x1, Pallas kernels, shards(): pl.pallas_call(kernel, out_shape=(side, side, wide, wide, tall, tall), in...  183 us
    mul x1, other arithmetic, shards(): outer_step = outer_rate * (mean_delta + momentum_rate * momentum_next)  6.42 us
    unnamed x17, local copies, waits for them, and re-layouts  5.02 us

profile of v2, /device:TPU:0, one launch (start us, length us, event | category | flops | bytes accessed | tf_op | source)
XLA Modules:
  0.0 195.0 jit_solution(18361479751465814343)
XLA Ops:
  0.6 0.0 copy-start
  0.6 182.8 %layer.1 = (bf16[128,512]{1,0:T(8,128)(2,1)}, bf16[128,512]{1,0:T(8,128)(2,1)}, bf16[512,1792]{1,0:T(8,128)(2,1)}, bf16[512,1792]{1,0:T(8,128)(2,1)}, bf16[1792,...) custom-call(bf16[128,512]{1,0:T(8,128)(2,1)} %bitcast.23, bf16[128,512]{1,0:T(8,128)(2,1)} %bitcast.24, ...), custom_call_target="tpu_custom_call" | custom-call | flops 16911433728 | bytes 16000000 | tf_op jit(solution)/shard_map/layer/pallas_call | solution.py:393
  183.5 0.0 copy-done
  183.5 0.0 copy-start.5
  183.5 0.0 copy-start.4
  183.5 0.0 copy-start.3
  183.5 6.4 %add_multiply_fusion = (f32[1792,512]{1,0:T(8,128)}, f32[1792,512]{1,0:T(8,128)}) fusion(bf16[1792,512]{1,0:T(8,128)(2,1)} %get-tuple-element.18, bf16[1,1792,512]{2,1,0:T(8,128)(2,1)} %param.12, f32[1792,512]{1,0:T(8,128)S(1)} %copy-done), kind=kLoop, calls=%fused_computation | loop fusion | flops 8257536 | bytes 14680064 | tf_op jit(solution)/shard_map/mul | solution.py:435
  189.9 0.0 copy-start.2
  189.9 0.0 copy-done.5
  190.0 0.7 copy.19
  190.6 0.0 copy-done.4
  190.6 0.7 copy.20
  191.3 0.0 copy-done.3
  191.3 0.0 copy-start.1
  191.3 1.2 copy.21
  192.5 0.0 copy-done.2
  192.5 1.2 copy.22
  193.7 0.0 copy-done.1
  193.7 1.2 copy.23
Async XLA Ops:
  0.6 182.9 %copy-start = (f32[1792,512]{1,0:T(8,128)S(1)}, f32[1792,512]{1,0:T(8,128)}, u32[]{:S(2)}) copy-start(f32[1792,512]{1,0:T(8,128)} %param.13) | copy-start | bytes 11010052
  183.5 6.5 %copy-start.5 = (bf16[128,512]{1,0:T(8,128)(2,1)S(1)}, bf16[128,512]{1,0:T(8,128)(2,1)}, u32[]{:S(2)}) copy-start(bf16[128,512]{1,0:T(8,128)(2,1)} %get-tuple-element.13) | copy-start | bytes 393220
  183.5 7.1 %copy-start.4 = (bf16[128,512]{1,0:T(8,128)(2,1)S(1)}, bf16[128,512]{1,0:T(8,128)(2,1)}, u32[]{:S(2)}) copy-start(bf16[128,512]{1,0:T(8,128)(2,1)} %get-tuple-element.14) | copy-start | bytes 393220
  183.5 7.8 %copy-start.3 = (bf16[512,1792]{1,0:T(8,128)(2,1)S(1)}, bf16[512,1792]{1,0:T(8,128)(2,1)}, u32[]{:S(2)}) copy-start(bf16[512,1792]{1,0:T(8,128)(2,1)} %get-tuple-element.15) | copy-start | bytes 5505028
  189.9 2.6 %copy-start.2 = (bf16[512,1792]{1,0:T(8,128)(2,1)S(1)}, bf16[512,1792]{1,0:T(8,128)(2,1)}, u32[]{:S(2)}) copy-start(bf16[512,1792]{1,0:T(8,128)(2,1)} %get-tuple-element.16) | copy-start | bytes 5505028
  191.3 2.5 %copy-start.1 = (bf16[1792,512]{1,0:T(8,128)(2,1)S(1)}, bf16[1792,512]{1,0:T(8,128)(2,1)}, u32[]{:S(2)}) copy-start(bf16[1792,512]{1,0:T(8,128)(2,1)} %get-tuple-element.17) | copy-start | bytes 5505028

commit v3 on v2

--- a/solution.py
+++ b/solution.py
@@ -1,5 +1,3 @@
-import functools
-
 import jax
 import jax.numpy as jnp
 from jax import lax
@@ -17,23 +15,26 @@
 OWN = 128
 DIM = 512
 UNITS = 1792
-SIZES = (128, 256, 256, 256, 128)
-STARTS = (0, 128, 384, 640, 896)
-CHUNKS = len(SIZES)
-SLOTS = 2
+CHUNKS = 8
+SLOTS = 3
 CY = 1024
 CX = UNITS - CY
 HY = CY // 2
 HX = CX // 2
+YB = OWN // 4
+XR = OWN // 2
+XB = XR // 4
 TILE = 256
-SEMS = 224
+SEMS = 342
 
 ORDER = (
-    "A0", "By0", "Bx0", "Bz0", "M0", "Cy0", "Cx0", "Dx0", "Dy0", "A1", "Ex0", "Ey0", "A2", "By1", "Bx1", "Fx0",
-    "Bz1", "Fy0", "By2", "Bx2", "Cy1", "Bz2", "Cx1", "A3", "G0", "Dy1", "Cy2", "Cx2", "A4", "Bx3", "Dx1", "By3",
-    "Bz3", "Dx2", "Ey1", "By4", "Cx3", "Dy2", "Bx4", "Ex1", "Bz4", "Cy3", "Ex2", "Ey2", "Fy1", "Cy4", "Dx3", "Cx4",
-    "Fx1", "Dy3", "Fx2", "Dy4", "Fy2", "G1", "Ex3", "Dx4", "Ey3", "G2", "Fx3", "Ey4", "Ex4", "Fy3", "Fy4", "Fx4",
-    "G3", "G4",
+    "A0", "By0", "M0", "A1", "Bx0", "Cy0", "Bz0", "By1", "Bx1", "A2", "Cx0", "A3", "Bz1", "Cx1", "Cy1", "By2",
+    "Dy0", "A4", "Dx0", "Bx2", "By3", "Bz2", "Bx3", "Dx1", "Cy2", "Bz3", "By4", "Dy1", "Ex0", "Ey0", "Cx2",
+    "A5", "Bx4", "Cy3", "Cx3", "A6", "Ex1", "Bz4", "Cy4", "Fx0", "Dy2", "Fy0", "Ey1", "Dx2", "By5", "Bx5",
+    "Cx4", "A7", "Dx3", "Bz5", "By6", "Fx1", "Dy3", "Bx6", "Bz6", "Fy1", "Ex2", "Cy5", "Cx5", "Dy4", "Dx4",
+    "G0", "By7", "Ey2", "Ex3", "Bx7", "Cy6", "Cx6", "Bz7", "Fx2", "Dx5", "G1", "W1", "Ey3", "Ex4", "Cy7", "Dy5",
+    "Fy2", "Fx3", "Cx7", "Ey4", "Dx6", "Ex5", "Dy6", "Fy3", "Fx4", "G2", "Dx7", "Fy4", "Dy7", "Ex6", "Fx5",
+    "Ey5", "G3", "Ex7", "Fx6", "Ey6", "G4", "Fx7", "Fy5", "Ey7", "Fy6", "G5", "W5", "Fy7", "G6", "G7", "X0",
 )
 
 
@@ -53,7 +54,7 @@
 def kernel(
     tok_in, cot_in, wg_hbm, wu_hbm, wd_hbm, frag_in,
     mixed_out, ig_out, gg_out, ug_out, dg_out, frag_out,
-    wg, wu, wd, tc_all, tc_t, part, h_all, ra, rb, sy, rc, e_own, xa, xb, xc, g_all, ms, ml, own, rz, rx, gg, ug, dg,
+    wg, wu, wd, tc_all, tc_t, part, h_all, ra, rb, sy, rc, e_own, xa, xb, xc, g_all, ms, ml, own, rz, rx, gg, ug, dt, dg,
     send_sem, recv_sem, local_sem,
 ):
     rep, d, t = lax.axis_index("replica"), lax.axis_index("dp"), lax.axis_index("tensor")
@@ -116,8 +117,7 @@
     pl.semaphore_wait(barrier, len(peers))
 
     mate = remote(tc_all.at[:, own_rows], tc_all.at[:, own_rows], to_xl)
-    z_targets = (to_zp, to_zm, to_zo)
-    gathers = [[remote(tc_all.at[:, own_rows], tc_all.at[:, own_rows], target)] for target in z_targets]
+    gathers = {}
     frag_copy = remote(frag_in, frag_out, to_core)
     for load in loads:
         load.wait()
@@ -125,63 +125,62 @@
     live = [dict() for _ in range(CHUNKS)]
 
     def row0(c, side):
-        if c in (1, 2, 3):
-            return (zm, zp, zo)[c - 1] * 2 * OWN
-        return (2 * z + (side if c == 0 else 1 - side)) * OWN
-
-    def y_rows(c, blk, base=0):
-        return rows_of(base + blk * (SIZES[c] // 4), SIZES[c] // 4)
-
-    def x_rows(c, blk, base=0):
-        return rows_of(base + blk * (SIZES[c] // 8), SIZES[c] // 8)
+        zz = (z, z, zm, zp, zo, zo, zm, zp)[c]
+        return (2 * zz + (1 - side if c in (1, 2, 3, 5) else side)) * OWN
+
+    def y_rows(blk, base=0):
+        return rows_of(base + blk * YB, YB)
+
+    def x_rows(blk, base=0):
+        return rows_of(base + blk * XB, XB)
 
     def y_own(c):
-        return pl.ds(STARTS[c] // 4, SIZES[c] // 4)
+        return pl.ds(c * YB, YB)
 
     def x_own(c):
-        return pl.ds(STARTS[c] // 8, SIZES[c] // 8)
+        return pl.ds(c * XB, XB)
 
     def xa_rows(c, blk):
-        return x_rows(c, blk, STARTS[c] // 2)
+        return x_rows(blk, c * XR)
 
     def stage_m(c):
         mate.wait_recv()
-        for k, target in enumerate(z_targets):
-            gathers[k].append(remote(tc_all.at[:, mate_rows], tc_all.at[:, mate_rows], target))
+        for chunks, place in (((3, 2), mate_rows), ((4,), own_rows), ((5,), mate_rows), ((7, 6), own_rows)):
+            for chunk in chunks:
+                target = {2: to_zp, 6: to_zp, 3: to_zm, 7: to_zm, 4: to_zo, 5: to_zo}[chunk]
+                gathers[chunk] = remote(tc_all.at[:, place], tc_all.at[:, place], target)
 
     def stage_a(c):
-        s, size, me = c % SLOTS, SIZES[c], live[c]
-        if c in (1, 2, 3):
-            for copy in gathers[c - 1]:
-                copy.wait_recv()
+        s, me = c % SLOTS, live[c]
+        if c in gathers:
+            gathers[c].wait_recv()
         if c >= SLOTS:
             for copy in live[c - SLOTS]["part_sends"]:
                 wait_sent(copy)
-        rows = rows_of(row0(c, xl), size, OWN)
-        kept = pl.ds(0, size)
+        rows = rows_of(row0(c, xl), OWN, OWN)
 
         def tile(k, carry):
             cols = pl.ds(pl.multiple_of(k * TILE, TILE), TILE)
             tok, cot = tc_all[0, rows, :], tc_all[1, rows, :]
-            part[s, 0, kept, cols] = dot(tok, wg[:, cols]).astype(BF16)
-            part[s, 1, kept, cols] = dot(tok, wu[:, cols]).astype(BF16)
-            part[s, 2, kept, cols] = dot(cot, wd[cols, :], 1, 1).astype(BF16)
+            part[s, 0, :, cols] = dot(tok, wg[:, cols]).astype(BF16)
+            part[s, 1, :, cols] = dot(tok, wu[:, cols]).astype(BF16)
+            part[s, 2, :, cols] = dot(cot, wd[cols, :], 1, 1).astype(BF16)
             return carry
 
         lax.fori_loop(0, CY // TILE, tile, 0)
         ps = part.at[s]
         first, second = pl.ds(0, HY), pl.ds(HY, HY)
         me["s1"] = [
-            remote(ps.at[:, y_rows(c, yo), first], ra.at[0, :, y_own(c)], to_yp),
-            remote(ps.at[:, y_rows(c, yo), second], ra.at[1, :, y_own(c)], to_ym),
-            remote(ps.at[:, y_rows(c, yp), second], rb.at[0, :, y_own(c), second], to_yp),
-            remote(ps.at[:, y_rows(c, ym), first], rb.at[1, :, y_own(c), first], to_ym),
+            remote(ps.at[:, y_rows(yo), first], ra.at[0, :, y_own(c)], to_yp),
+            remote(ps.at[:, y_rows(yo), second], ra.at[1, :, y_own(c)], to_ym),
+            remote(ps.at[:, y_rows(yp), second], rb.at[0, :, y_own(c), second], to_yp),
+            remote(ps.at[:, y_rows(ym), first], rb.at[1, :, y_own(c), first], to_ym),
         ]
         lax.fori_loop(CY // TILE, UNITS // TILE, tile, 0)
         me["t1"] = []
         for blk in (yo, yp, ym, y):
             for k, (half, target) in enumerate(((hp, to_xp), (hm, to_xm))):
-                src = ps.at[:, x_rows(c, blk, half * (size // 2)), pl.ds(CY, CX)]
+                src = ps.at[:, x_rows(blk, half * XR), pl.ds(CY, CX)]
                 me["t1"].append(remote(src, xa.at[k, :, xa_rows(c, blk)], target))
         me["part_sends"] = me["s1"] + me["t1"]
         for k in range(2):
@@ -191,7 +190,7 @@
         s, me = c % SLOTS, live[c]
         me["s2"] = []
         for k, (blk, target) in enumerate(((yp, to_yp), (ym, to_ym))):
-            rows, cols = y_rows(c, blk), pl.ds(k * HY, HY)
+            rows, cols = y_rows(blk), pl.ds(k * HY, HY)
             me["s1"][k].wait_recv()
             for a in range(3):
                 total = part[s, a, rows, cols].astype(F32) + ra[k, a, y_own(c), :].astype(F32)
@@ -229,7 +228,7 @@
         s, me = c % SLOTS, live[c]
         for copy in me["s1"][2:] + me["s2"]:
             copy.wait_recv()
-        rows, own = y_rows(c, y), y_own(c)
+        rows, own = y_rows(y), y_own(c)
         for h in range(2):
             cols = pl.ds(h * HY, HY)
             for a in range(3):
@@ -257,11 +256,11 @@
         sums = [rc[0, a, own, :].astype(F32) + rc[1, a, own, :].astype(F32) for a in range(3)]
         for a, value in enumerate(pointwise(*sums)):
             e_own[a, own, :] = value
-        place = h_all.at[:, y_rows(c, y, row0(c, 1 - xl)), pl.ds(pl.multiple_of(xh * HY, HY), HY)]
+        place = h_all.at[:, y_rows(y, row0(c, 1 - xl)), pl.ds(pl.multiple_of(xh * HY, HY), HY)]
         me["s4"] = [remote(e_own.at[:, own], place, target) for target in (to_xp, to_xm)]
 
     def send_x(c, blk):
-        place = h_all.at[:, x_rows(c, blk, row0(c, 1 - xl) + xh * (SIZES[c] // 2)), pl.ds(CY, CX)]
+        place = h_all.at[:, x_rows(blk, row0(c, 1 - xl) + xh * XR), pl.ds(CY, CX)]
         live[c]["t6"] += [remote(g_all.at[:, xa_rows(c, blk)], place, target) for target in (to_xp, to_xm)]
 
     def stage_dx(c):
@@ -284,7 +283,7 @@
         me = live[c]
         for copy in me["s4"]:
             copy.wait_recv()
-        place = h_all.at[:, y_rows(c, y, row0(c, xl)), pl.ds(0, CY)]
+        place = h_all.at[:, y_rows(y, row0(c, xl)), pl.ds(0, CY)]
         me["s5"] = [remote(place, place, target) for target in (to_yp, to_ym)]
 
     def stage_ex(c):
@@ -302,7 +301,7 @@
         me["s6"] = []
         for k, (blk, target) in enumerate(((ym, to_yp), (yp, to_ym))):
             me["s5"][k].wait_recv()
-            place = h_all.at[:, y_rows(c, blk, row0(c, xl)), pl.ds(k * HY, HY)]
+            place = h_all.at[:, y_rows(blk, row0(c, xl)), pl.ds(k * HY, HY)]
             me["s6"].append(remote(place, place, target))
 
     def stage_fx(c):
@@ -310,25 +309,21 @@
             copy.wait_recv()
         send_x(c, yo)
 
-    zsum = []
+    zsum = {}
     last = []
+    blocks = {2: 0, 3: 1, 5: 2, 4: 3, 6: 4, 7: 5}
 
     def stage_g(c):
         me = live[c]
         for copy in me["s6"] + me["t6"]:
             copy.wait_recv()
-        rows = rows_of(row0(c, xl), SIZES[c], OWN)
-        if c == 4:
-            for copy in zsum:
-                copy.wait_recv()
+        rows = rows_of(row0(c, xl), OWN, OWN)
 
         def keep(k, cols, value):
-            if c == 0:
-                own[k, :, cols] = value
-            elif c == 4:
-                ml[k, :, cols] = (value + z_sum(k, 1 - xl, cols)).astype(BF16)
+            if c < 2:
+                own[c, k, :, cols] = value
             else:
-                ms[c - 1, k, :, cols] = value.astype(BF16)
+                ms[blocks[c], k, :, cols] = value.astype(BF16)
 
         def mixed_tile(k, carry):
             cols = pl.ds(pl.multiple_of(k * TILE, TILE), TILE)
@@ -341,41 +336,75 @@
             keep(1, cols, term)
             return carry
 
+        zsum[c] = []
         for k, body in enumerate((mixed_tile, ig_tile)):
             lax.fori_loop(0, DIM // TILE, body, 0)
-            if c == 4:
-                last.append(remote(ml.at[k], rx.at[k], to_xl))
-        if c in (1, 2, 3):
-            zsum.append(remote(ms.at[c - 1], rz.at[c - 1], (to_zm, to_zp, to_zo)[c - 1]))
-
-    def z_sum(k, side, cols):
-        rows = rows_of(side * OWN, OWN, OWN)
-        total = rz[0, k, rows, cols].astype(F32) + rz[1, k, rows, cols].astype(F32)
-        return total + rz[2, k, rows, cols].astype(F32)
+            if c >= 2:
+                target = {2: to_zm, 6: to_zm, 3: to_zp, 7: to_zp, 4: to_zo, 5: to_zo}[c]
+                zsum[c].append(remote(ms.at[blocks[c], k], rz.at[blocks[c], k], target))
+
+    def z_sum(k, first):
+        total = rz[first, k].astype(F32) + rz[first + 1, k].astype(F32)
+        return total + rz[first + 2, k].astype(F32)
+
+    def stage_x(c):
+        for k in range(2):
+            for chunk in (2, 3, 5):
+                zsum[chunk][k].wait_recv()
+            ml[k] = (own[1, k] + z_sum(k, 0)).astype(BF16)
+            last.append(remote(ml.at[k], rx.at[k], to_xl))
+
+    def pair(zz):
+        return rows_of(2 * zz * OWN, 2 * OWN, 2 * OWN)
+
+    def grads(places, base, out):
+        def tile_of(which, a, base):
+            def tile(k, carry):
+                cols = pl.ds(pl.multiple_of(k * TILE, TILE), TILE)
+                total = None if base is None else base[:, cols].astype(F32)
+                for rows in places:
+                    term = dot(tc_t[which, :, rows], h_all[a, rows, cols])
+                    total = term if total is None else total + term
+                out(a, cols, total.astype(BF16))
+                return carry
+
+            return tile
+
+        for which, a, ref in ((0, 1, gg), (0, 2, ug), (1, 0, dt)):
+            lax.fori_loop(0, UNITS // TILE, tile_of(which, a, None if base is None else ref), 0)
+            yield a
+
+    def kept(a, cols, value):
+        {0: dt, 1: gg, 2: ug}[a][:, cols] = value
+
+    def stored(a, cols, value):
+        if a == 0:
+            dg[cols, :] = value.T
+        else:
+            kept(a, cols, value)
+
+    def stage_w(c):
+        for _ in grads([pair(z if c == 1 else zo)], None if c == 1 else True, kept):
+            pass
 
     stages = dict(
         A=stage_a, M=stage_m, By=stage_by, Bx=stage_bx, Bz=stage_bz, Cy=stage_cy, Cx=stage_cx, Dy=stage_dy,
-        Dx=stage_dx, Ey=stage_ey, Ex=stage_ex, Fy=stage_fy, Fx=stage_fx, G=stage_g,
+        Dx=stage_dx, Ey=stage_ey, Ex=stage_ex, Fy=stage_fy, Fx=stage_fx, G=stage_g, W=stage_w, X=stage_x,
     )
     for step in ORDER:
         stages[step[:-1]](int(step[-1]))
 
-    def grad_tile(k, carry):
-        cols = pl.ds(pl.multiple_of(k * TILE, TILE), TILE)
-        gg[:, cols] = dot(tc_t[0], h_all[1, :, cols]).astype(BF16)
-        ug[:, cols] = dot(tc_t[0], h_all[2, :, cols]).astype(BF16)
-        dg[cols, :] = dot(tc_t[1], h_all[0, :, cols]).astype(BF16).T
-        return carry
-
-    lax.fori_loop(0, UNITS // TILE, grad_tile, 0)
     stores = []
-    for k, (src, dst) in enumerate(((gg, gg_out), (ug, ug_out), (dg, dg_out))):
-        store = pltpu.make_async_copy(src, dst, local_sem.at[3 + k])
+    for a in grads([pair(zm), pair(zp)], True, stored):
+        src, dst = {0: (dg, dg_out), 1: (gg, gg_out), 2: (ug, ug_out)}[a]
+        store = pltpu.make_async_copy(src, dst, local_sem.at[3 + a])
         store.start()
         stores.append(store)
 
     for k, out in enumerate((mixed_out, ig_out)):
-        total = own[k] + z_sum(k, xl, pl.ds(0, DIM))
+        for chunk in (4, 6, 7):
+            zsum[chunk][k].wait_recv()
+        total = own[0, k] + z_sum(k, 3)
         last[k].wait_recv()
         out[...] = (total + rx[k].astype(F32)).astype(BF16)
     frag_copy.wait_recv()
@@ -401,7 +430,7 @@
             pltpu.VMEM((UNITS, DIM), BF16),
             pltpu.VMEM((2, ROWS, DIM), BF16),
             pltpu.VMEM((2, DIM, ROWS), BF16),
-            pltpu.VMEM((SLOTS, 3, max(SIZES), UNITS), BF16),
+            pltpu.VMEM((SLOTS, 3, OWN, UNITS), BF16),
             pltpu.VMEM((3, ROWS, UNITS), BF16),
             pltpu.VMEM((2, 3, ROWS // 4, HY), BF16),
             pltpu.VMEM((2, 3, ROWS // 4, CY), BF16),
@@ -412,11 +441,12 @@
             pltpu.VMEM((2, 3, ROWS // 8, HX), BF16),
             pltpu.VMEM((2, 3, ROWS // 8, CX), BF16),
             pltpu.VMEM((3, ROWS // 2, CX), BF16),
-            pltpu.VMEM((3, 2, 2 * OWN, DIM), BF16),
+            pltpu.VMEM((6, 2, OWN, DIM), BF16),
             pltpu.VMEM((2, OWN, DIM), BF16),
-            pltpu.VMEM((2, OWN, DIM), F32),
-            pltpu.VMEM((3, 2, 2 * OWN, DIM), BF16),
+            pltpu.VMEM((2, 2, OWN, DIM), F32),
+            pltpu.VMEM((6, 2, OWN, DIM), BF16),
             pltpu.VMEM((2, OWN, DIM), BF16),
+            pltpu.VMEM((DIM, UNITS), BF16),
             pltpu.VMEM((DIM, UNITS), BF16),
             pltpu.VMEM((DIM, UNITS), BF16),
             pltpu.VMEM((UNITS, DIM), BF16),
@@ -425,7 +455,7 @@
             pltpu.SemaphoreType.DMA((6,)),
         ],
         compiler_params=pltpu.CompilerParams(
-            collective_id=0, has_side_effects=True, vmem_limit_bytes=60 * 1024 * 1024
+            collective_id=0, has_side_effects=True, vmem_limit_bytes=56 * 1024 * 1024
         ),
         cost_estimate=pl.CostEstimate(flops=18 * ROWS * DIM * UNITS, bytes_accessed=16_000_000, transcendentals=0),
         name="layer",

time: 196 us -> 187 us (0.954)
  Pallas kernels: 183 us -> 176 us
    pallas_call x1, Pallas kernels: 183 us -> 176 us  [shards(): pl.pallas_call(kernel, out_shape=(side, side, wide, wide, tall, tall), in...]
    unnamed x17 -> x19, local copies, waits for them, and re-layouts: 5.02 us -> 5.02 us
where the time goes in v3:
time: 187 us
  Pallas kernels  176 us (94%)
  other arithmetic  5.87 us (3%)
  local copies, waits for them, and re-layouts  5.02 us (3%)
    pallas_call x1, Pallas kernels, shards(): pl.pallas_call(kernel, out_shape=(side, side, wide, wide, tall, tall), in...  176 us
    mul x1, other arithmetic, shards(): outer_step = outer_rate * (mean_delta + momentum_rate * momentum_next)  5.87 us
    unnamed x19, local copies, waits for them, and re-layouts  5.02 us

profile of v3, /device:TPU:0, one launch (start us, length us, event | category | flops | bytes accessed | tf_op | source)
XLA Modules:
  0.0 187.4 jit_solution(7438423543916214212)
XLA Ops:
  0.6 0.0 copy-start
  0.6 0.0 copy-start.1
  0.7 175.8 %layer.1 = (bf16[128,512]{1,0:T(8,128)(2,1)}, bf16[128,512]{1,0:T(8,128)(2,1)}, bf16[512,1792]{1,0:T(8,128)(2,1)}, bf16[512,1792]{1,0:T(8,128)(2,1)}, bf16[1792,...) custom-call(bf16[128,512]{1,0:T(8,128)(2,1)} %bitcast.23, bf16[128,512]{1,0:T(8,128)(2,1)} %bitcast.24, ...), custom_call_target="tpu_custom_call" | custom-call | flops 16911433728 | bytes 16000000 | tf_op jit(solution)/shard_map/layer/pallas_call | solution.py:422
  176.4 0.0 copy-done
  176.4 0.0 copy-done.1
  176.4 0.0 copy-start.6
  176.4 0.0 copy-start.5
  176.5 0.0 copy-start.4
  176.5 5.9 %add_multiply_fusion = (f32[1792,512]{1,0:T(8,128)}, f32[1792,512]{1,0:T(8,128)}) fusion(bf16[1792,512]{1,0:T(8,128)(2,1)} %get-tuple-element.18, bf16[1,1792,512]{2,1,0:T(8,128)(2,1)S(1)} %copy-done.1, f32[1792,512]{1,0:T(8,128)S(1)} %copy-done), kind=kLoop, calls=%fused_computation | loop fusion | flops 8257536 | bytes 14680064 | tf_op jit(solution)/shard_map/mul | solution.py:465
  182.3 0.0 copy-start.3
  182.3 0.0 copy-done.6
  182.3 0.7 copy.19
  183.0 0.0 copy-done.5
  183.0 0.7 copy.20
  183.7 0.0 copy-done.4
  183.7 0.0 copy-start.2
  183.7 1.2 copy.21
  184.9 0.0 copy-done.3
  184.9 1.2 copy.22
  186.1 0.0 copy-done.2
  186.1 1.2 copy.23
Async XLA Ops:
  0.6 175.8 %copy-start = (f32[1792,512]{1,0:T(8,128)S(1)}, f32[1792,512]{1,0:T(8,128)}, u32[]{:S(2)}) copy-start(f32[1792,512]{1,0:T(8,128)} %param.13) | copy-start | bytes 11010052
  0.6 175.8 %copy-start.1 = (bf16[1,1792,512]{2,1,0:T(8,128)(2,1)S(1)}, bf16[1,1792,512]{2,1,0:T(8,128)(2,1)}, u32[]{:S(2)}) copy-start(bf16[1,1792,512]{2,1,0:T(8,128)(2,1)} %param.12) | copy-start | bytes 5505028
  176.4 5.9 %copy-start.6 = (bf16[128,512]{1,0:T(8,128)(2,1)S(1)}, bf16[128,512]{1,0:T(8,128)(2,1)}, u32[]{:S(2)}) copy-start(bf16[128,512]{1,0:T(8,128)(2,1)} %get-tuple-element.13) | copy-start | bytes 393220
  176.4 6.6 %copy-start.5 = (bf16[128,512]{1,0:T(8,128)(2,1)S(1)}, bf16[128,512]{1,0:T(8,128)(2,1)}, u32[]{:S(2)}) copy-start(bf16[128,512]{1,0:T(8,128)(2,1)} %get-tuple-element.14) | copy-start | bytes 393220
  176.5 7.2 %copy-start.4 = (bf16[512,1792]{1,0:T(8,128)(2,1)S(1)}, bf16[512,1792]{1,0:T(8,128)(2,1)}, u32[]{:S(2)}) copy-start(bf16[512,1792]{1,0:T(8,128)(2,1)} %get-tuple-element.15) | copy-start | bytes 5505028
  182.3 2.6 %copy-start.3 = (bf16[512,1792]{1,0:T(8,128)(2,1)S(1)}, bf16[512,1792]{1,0:T(8,128)(2,1)}, u32[]{:S(2)}) copy-start(bf16[512,1792]{1,0:T(8,128)(2,1)} %get-tuple-element.16) | copy-start | bytes 5505028
  183.7 2.5 %copy-start.2 = (bf16[1792,512]{1,0:T(8,128)(2,1)S(1)}, bf16[1792,512]{1,0:T(8,128)(2,1)}, u32[]{:S(2)}) copy-start(bf16[1792,512]{1,0:T(8,128)(2,1)} %get-tuple-element.17) | copy-start | bytes 5505028

commit v4 on v3

--- a/solution.py
+++ b/solution.py
@@ -16,7 +16,7 @@
 DIM = 512
 UNITS = 1792
 CHUNKS = 8
-SLOTS = 3
+SLOTS = 4
 CY = 1024
 CX = UNITS - CY
 HY = CY // 2
@@ -28,13 +28,13 @@
 SEMS = 342
 
 ORDER = (
-    "A0", "By0", "M0", "A1", "Bx0", "Cy0", "Bz0", "By1", "Bx1", "A2", "Cx0", "A3", "Bz1", "Cx1", "Cy1", "By2",
-    "Dy0", "A4", "Dx0", "Bx2", "By3", "Bz2", "Bx3", "Dx1", "Cy2", "Bz3", "By4", "Dy1", "Ex0", "Ey0", "Cx2",
-    "A5", "Bx4", "Cy3", "Cx3", "A6", "Ex1", "Bz4", "Cy4", "Fx0", "Dy2", "Fy0", "Ey1", "Dx2", "By5", "Bx5",
-    "Cx4", "A7", "Dx3", "Bz5", "By6", "Fx1", "Dy3", "Bx6", "Bz6", "Fy1", "Ex2", "Cy5", "Cx5", "Dy4", "Dx4",
-    "G0", "By7", "Ey2", "Ex3", "Bx7", "Cy6", "Cx6", "Bz7", "Fx2", "Dx5", "G1", "W1", "Ey3", "Ex4", "Cy7", "Dy5",
-    "Fy2", "Fx3", "Cx7", "Ey4", "Dx6", "Ex5", "Dy6", "Fy3", "Fx4", "G2", "Dx7", "Fy4", "Dy7", "Ex6", "Fx5",
-    "Ey5", "G3", "Ex7", "Fx6", "Ey6", "G4", "Fx7", "Fy5", "Ey7", "Fy6", "G5", "W5", "Fy7", "G6", "G7", "X0",
+    "A0", "By0", "M0", "A1", "Bx0", "Bz0", "Cy0", "A2", "By1", "Bx1", "A3", "Cx0", "Bz1", "A4", "Dy0", "By2",
+    "Bx2", "Cy1", "Cx1", "A5", "Bz2", "By3", "Bx3", "Dx0", "Bz3", "By4", "Bx4", "Cy2", "Cx2", "Bz4", "A6",
+    "Dx1", "By5", "Ey0", "Dy1", "Bx5", "Cy3", "Cx3", "A7", "Bz5", "Ex0", "Cy4", "Cx4", "Dx2", "Dy2", "Bx6",
+    "By6", "Bz6", "Ex1", "Cy5", "Ey1", "Fy0", "Dy3", "Cx5", "Dx3", "Bx7", "By7", "Bz7", "Fx0", "Dx4", "Ex2",
+    "Cx6", "Dy4", "Cy6", "Fx1", "Ey2", "Fy1", "Dy5", "Dx5", "Ex3", "Ey3", "Cx7", "Cy7", "G0", "Ex4", "Fx2",
+    "Dx6", "Ey4", "Fy2", "Dy6", "G1", "W1", "Ex5", "Ey5", "Fx3", "Fy3", "Dx7", "Fx4", "Dy7", "Ex6", "Fy4", "G2",
+    "Fx5", "Ey6", "Fy5", "G3", "Ex7", "Fx6", "G4", "Ey7", "Fy6", "G5", "W5", "Fx7", "Fy7", "G6", "G7", "X0",
 )
 
 

time: 187 us -> 186 us (level)
  no operation moved by 1% of the time
where the time goes in v4:
time: 186 us
  Pallas kernels  175 us (94%)
  other arithmetic  5.87 us (3%)
  local copies, waits for them, and re-layouts  5.02 us (3%)
    pallas_call x1, Pallas kernels, shards(): pl.pallas_call(kernel, out_shape=(side, side, wide, wide, tall, tall), in...  175 us
    mul x1, other arithmetic, shards(): outer_step = outer_rate * (mean_delta + momentum_rate * momentum_next)  5.87 us
    unnamed x19, local copies, waits for them, and re-layouts  5.02 us

profile of v4, /device:TPU:0, one launch (start us, length us, event | category | flops | bytes accessed | tf_op | source)
XLA Modules:
  0.0 186.3 jit_solution(16781535192580040086)
XLA Ops:
  0.6 0.0 copy-start
  0.6 0.0 copy-start.1
  0.7 174.7 %layer.1 = (bf16[128,512]{1,0:T(8,128)(2,1)}, bf16[128,512]{1,0:T(8,128)(2,1)}, bf16[512,1792]{1,0:T(8,128)(2,1)}, bf16[512,1792]{1,0:T(8,128)(2,1)}, bf16[1792,...) custom-call(bf16[128,512]{1,0:T(8,128)(2,1)} %bitcast.23, bf16[128,512]{1,0:T(8,128)(2,1)} %bitcast.24, ...), custom_call_target="tpu_custom_call" | custom-call | flops 16911433728 | bytes 16000000 | tf_op jit(solution)/shard_map/layer/pallas_call | solution.py:422
  175.4 0.0 copy-done
  175.4 0.0 copy-done.1
  175.4 0.0 copy-start.6
  175.4 0.0 copy-start.5
  175.4 0.0 copy-start.4
  175.4 5.9 %add_multiply_fusion = (f32[1792,512]{1,0:T(8,128)}, f32[1792,512]{1,0:T(8,128)}) fusion(bf16[1792,512]{1,0:T(8,128)(2,1)} %get-tuple-element.18, bf16[1,1792,512]{2,1,0:T(8,128)(2,1)S(1)} %copy-done.1, f32[1792,512]{1,0:T(8,128)S(1)} %copy-done), kind=kLoop, calls=%fused_computation | loop fusion | flops 8257536 | bytes 14680064 | tf_op jit(solution)/shard_map/mul | solution.py:465
  181.3 0.0 copy-start.3
  181.3 0.0 copy-done.6
  181.3 0.7 copy.19
  181.9 0.0 copy-done.5
  181.9 0.7 copy.20
  182.6 0.0 copy-done.4
  182.6 0.0 copy-start.2
  182.6 1.2 copy.21
  183.8 0.0 copy-done.3
  183.8 1.2 copy.22
  185.1 0.0 copy-done.2
  185.1 1.2 copy.23
Async XLA Ops:
  0.6 174.7 %copy-start = (f32[1792,512]{1,0:T(8,128)S(1)}, f32[1792,512]{1,0:T(8,128)}, u32[]{:S(2)}) copy-start(f32[1792,512]{1,0:T(8,128)} %param.13) | copy-start | bytes 11010052
  0.6 174.7 %copy-start.1 = (bf16[1,1792,512]{2,1,0:T(8,128)(2,1)S(1)}, bf16[1,1792,512]{2,1,0:T(8,128)(2,1)}, u32[]{:S(2)}) copy-start(bf16[1,1792,512]{2,1,0:T(8,128)(2,1)} %param.12) | copy-start | bytes 5505028
  175.4 5.9 %copy-start.6 = (bf16[128,512]{1,0:T(8,128)(2,1)S(1)}, bf16[128,512]{1,0:T(8,128)(2,1)}, u32[]{:S(2)}) copy-start(bf16[128,512]{1,0:T(8,128)(2,1)} %get-tuple-element.13) | copy-start | bytes 393220
  175.4 6.6 %copy-start.5 = (bf16[128,512]{1,0:T(8,128)(2,1)S(1)}, bf16[128,512]{1,0:T(8,128)(2,1)}, u32[]{:S(2)}) copy-start(bf16[128,512]{1,0:T(8,128)(2,1)} %get-tuple-element.14) | copy-start | bytes 393220
  175.4 7.2 %copy-start.4 = (bf16[512,1792]{1,0:T(8,128)(2,1)S(1)}, bf16[512,1792]{1,0:T(8,128)(2,1)}, u32[]{:S(2)}) copy-start(bf16[512,1792]{1,0:T(8,128)(2,1)} %get-tuple-element.15) | copy-start | bytes 5505028
  181.3 2.6 %copy-start.3 = (bf16[512,1792]{1,0:T(8,128)(2,1)S(1)}, bf16[512,1792]{1,0:T(8,128)(2,1)}, u32[]{:S(2)}) copy-start(bf16[512,1792]{1,0:T(8,128)(2,1)} %get-tuple-element.16) | copy-start | bytes 5505028
  182.6 2.5 %copy-start.2 = (bf16[1792,512]{1,0:T(8,128)(2,1)S(1)}, bf16[1792,512]{1,0:T(8,128)(2,1)}, u32[]{:S(2)}) copy-start(bf16[1792,512]{1,0:T(8,128)(2,1)} %get-tuple-element.17) | copy-start | bytes 5505028
